TPU v7x, 128 devices: a whole 4x4x4 slice. The times are simulated.
128 devices in a mesh: rows: 16 (over x_hi, y, core), ctx: 8 (over x_lo, z).
Axes of the slice: x: 4 (x_hi: 2, x_lo: 2; x = x_hi * 2 + x_lo), y: 4, z: 4, core: 2. Of those that a mesh axis runs over, the one named last changes fastest.
Arguments:
- tokens: bfloat16 [2, 16, 1024, 1024], P(None, 'rows', 'ctx'), may hold values from -6 to 6
- cotangent: bfloat16 [2, 16, 1024, 1024], P(None, 'rows', 'ctx'), may hold values from -6 to 6
- bounds: int32 [2, 16, 5], P(None, 'rows'), may hold values from 0 to 1024, as said below
- positions: int32 [2, 16, 1024], P(None, 'rows', 'ctx'), may hold values from 0 to 1023, as said below
- norm_gain_attn: float32 [1024], replicated, may hold values from 0.5 to 1.5
- w_qkv: bfloat16 [1024, 2048], replicated, may hold values from -0.1875 to 0.1875
- qk_gain: float32 [128], replicated, may hold values from 0.5 to 1.5
- w_out: bfloat16 [1024, 1024], replicated, may hold values from -0.75 to 0.75
- norm_gain_ffn: float32 [1024], replicated, may hold values from 0.5 to 1.5
- w_gate_up: bfloat16 [1024, 9216], replicated, may hold values from -0.1875 to 0.1875
- w_down: bfloat16 [4608, 1024], replicated, may hold values from -0.09375 to 0.09375
Outputs:
- layer_out: bfloat16 [2, 16, 1024, 1024], P(None, 'rows', 'ctx')
- grad_tokens: float32 [2, 16, 1024, 1024], P(None, 'rows', 'ctx')
- grad_norm_attn: float32 [1024], P(('rows', 'ctx'))
- grad_qkv: float32 [1024, 2048], P(('rows', 'ctx'))
- grad_qk_gain: float32 [128], P(('rows', 'ctx'))
- grad_out: float32 [1024, 1024], P(('rows', 'ctx'))
- grad_norm_ffn: float32 [1024], P(('rows', 'ctx'))
- grad_gate_up: float32 [1024, 9216], P(('rows', 'ctx'))
- grad_down: float32 [4608, 1024], P(('rows', 'ctx'))
Inputs may be any that keep to these rules, and one draw needn't show every extreme that they name: `bounds`: in each row the offsets rise strictly; the first is 0 and the last is 1024; document k holds the tokens from offset k up to offset k + 1. `positions`: within a document the position rises by one from token to token.
All inputs are finite; a program needn't handle non-finite values.
Results may differ from a plain program's by a relative error of at most 0.035.
Values may be sent and summed in bfloat16 or wider, within the bound.
A program may use at most 256 MiB of HBM per device.

v0:
```python
import functools

import jax
import jax.numpy as jnp
import numpy as np
from jax import lax
from jax.experimental import pallas as pl
from jax.experimental.pallas import tpu as pltpu
from jax.sharding import PartitionSpec as P

MESH = pl.DeviceIdType.MESH
norm_eps = 1e-05
rope_theta = 1000000.0
f32 = jnp.float32
bf16 = jnp.bfloat16
VMEM_LIMIT = 64 * 2**20 - 2**18


class Place:
    def __init__(self):
        r = lax.axis_index("rows")
        k = lax.axis_index("ctx")
        self.x_hi = lax.div(r, 8)
        self.y = lax.rem(lax.div(r, 2), 4)
        self.core = lax.rem(r, 2)
        self.x_lo = lax.div(k, 4)
        self.z = lax.rem(k, 4)
        self.rows = r
        self.ctx = k
        self.bits = [
            self.x_hi,
            lax.rem(self.x_hi + self.x_lo, 2),
            lax.div(self.y, 2),
            lax.rem(lax.div(self.y, 2) + lax.rem(self.y, 2), 2),
            lax.div(self.z, 2),
            lax.rem(lax.div(self.z, 2) + lax.rem(self.z, 2), 2),
        ]

    def at(self, x_hi=None, x_lo=None, y=None, z=None, core=None):
        x_hi = self.x_hi if x_hi is None else x_hi
        x_lo = self.x_lo if x_lo is None else x_lo
        y = self.y if y is None else y
        z = self.z if z is None else z
        core = self.core if core is None else core
        return (x_hi * 8 + y * 2 + core, x_lo * 4 + z)

    def partner(self):
        return self.at(core=1 - self.core)

    def neighbour(self, dim):
        if dim == 0:
            return self.at(x_hi=1 - self.x_hi, x_lo=1 - self.x_lo)
        if dim == 1:
            return self.at(x_lo=1 - self.x_lo)
        if dim == 2:
            return self.at(y=3 - self.y)
        if dim == 3:
            return self.at(y=self.y + 1 - 2 * lax.rem(self.y, 2))
        if dim == 4:
            return self.at(z=3 - self.z)
        return self.at(z=self.z + 1 - 2 * lax.rem(self.z, 2))


def gray(v):
    return v ^ (v >> 1)


def chip_number(x_hi, x_lo, y, z):
    return gray(2 * x_hi + x_lo) * 16 + gray(y) * 4 + gray(z)


def slot_of(number, order):
    return sum(((number >> (5 - dim)) & 1) << (5 - t) for t, dim in enumerate(order))


HELD_AT = [64 - (64 >> t) for t in range(7)]


class Scatter:
    def __init__(self, place, orders, first, held, send_sems, recv_sems):
        self.place = place
        self.orders = orders
        self.first, self.first_cols = first
        self.held, self.held_cols = held
        self.send_sems = send_sems
        self.recv_sems = recv_sems

    def part(self, s, t, which):
        half = 32 >> t
        if t == 0:
            return self.first, which * half, self.first_cols
        return self.held, HELD_AT[t - 1] + which * half, self.held_cols

    def copy(self, s, t):
        half = 32 >> t
        dim = self.orders[s][t]
        ref, start, cols = self.part(s, t, 1 - self.place.bits[dim])
        return pltpu.make_async_remote_copy(
            src_ref=ref.at[s, pl.ds(start, half), :, cols],
            dst_ref=self.held.at[s, pl.ds(HELD_AT[t], half), :, self.held_cols],
            send_sem=self.send_sems.at[s, t],
            recv_sem=self.recv_sems.at[s, t],
            device_id=self.place.neighbour(dim),
            device_id_type=MESH,
        )

    def send(self, s, t):
        self.copy(s, t).start()

    def take(self, s, t):
        self.copy(s, t).wait_recv()
        half = 32 >> t
        ref, start, cols = self.part(s, t, self.place.bits[self.orders[s][t]])
        per = min(8, half)

        def body(i, carry):
            for j in range(per):
                at = i * per + j
                self.held[s, HELD_AT[t] + at, :, self.held_cols] = (
                    self.held[s, HELD_AT[t] + at, :, self.held_cols].astype(f32)
                    + ref[s, start + at, :, cols].astype(f32)
                ).astype(bf16)
            return carry

        lax.fori_loop(0, half // per, body, 0)
        self.send(s, t + 1)

    def last(self, s):
        self.copy(s, 5).wait_recv()
        ref, start, cols = self.part(s, 5, self.place.bits[self.orders[s][5]])
        return self.held[s, HELD_AT[5], :, self.held_cols].astype(f32) + ref[
            s, start, :, cols
        ].astype(f32)

    def sent(self, steps=range(6)):
        for s in range(6):
            for t in steps:
                self.copy(s, t).wait_send()


def greet(devices):
    barrier = pltpu.get_barrier_semaphore()
    for device in devices:
        pl.semaphore_signal(barrier, inc=1, device_id=device, device_id_type=MESH)
    pl.semaphore_wait(barrier, len(devices))


def greet_all(place, devices):
    barrier = pltpu.get_barrier_semaphore()
    targets = down_targets(place)
    for device in devices + targets[1:]:
        pl.semaphore_signal(barrier, inc=1, device_id=device, device_id_type=MESH)
    swapped = place.x_hi != place.core
    count = len(devices) + 3

    @pl.when(swapped)
    def _():
        pl.semaphore_signal(barrier, inc=1, device_id=targets[0], device_id_type=MESH)
        pl.semaphore_wait(barrier, count + 1)

    @pl.when(jnp.logical_not(swapped))
    def _():
        pl.semaphore_wait(barrier, count)


def push(place, src, dst, send_sem, recv_sem, device):
    return pltpu.make_async_remote_copy(
        src_ref=src,
        dst_ref=dst,
        send_sem=send_sem,
        recv_sem=recv_sem,
        device_id=device,
        device_id_type=MESH,
    )


def down_targets(place):
    return [
        place.at(x_hi=place.core, core=place.x_hi, z=lax.rem(place.z + off, 4)) for off in range(4)
    ]


def dot(left, right):
    return jnp.dot(left, right, preferred_element_type=f32)


def dot_cols(left, right):
    return lax.dot_general(left, right, (((1,), (1,)), ((), ())), preferred_element_type=f32)


FF_HALF = 2304
DOWN_ORDERS = (
    (1, 3, 5, 2, 0, 4),
    (4, 0, 1, 3, 5, 2),
    (0, 1, 3, 2, 4, 5),
    (5, 3, 0, 1, 2, 4),
    (3, 2, 4, 5, 1, 0),
    (2, 3, 5, 0, 4, 1),
)
GATE_ORDERS = (
    (0, 5, 4, 1, 3, 2),
    (1, 5, 0, 4, 3, 2),
    (2, 4, 5, 3, 1, 0),
    (3, 0, 5, 4, 2, 1),
    (2, 5, 0, 3, 1, 4),
    (0, 1, 3, 4, 5, 2),
)
UP_ORDERS = (
    (2, 0, 3, 5, 1, 4),
    (5, 2, 0, 3, 4, 1),
    (3, 1, 5, 2, 0, 4),
    (4, 2, 5, 0, 1, 3),
    (3, 0, 2, 5, 4, 1),
    (4, 1, 5, 0, 2, 3),
)
QUAD_ORDERS = (
    (1, 2, 0, 5, 4, 3),
    (0, 4, 1, 2, 3, 5),
    (3, 1, 5, 0, 2, 4),
    (2, 0, 3, 4, 1, 5),
    (2, 4, 3, 5, 0, 1),
    (4, 0, 2, 3, 5, 1),
)
STEPS = (
    "Bmm0", "Amm0", "Bmm2", "dn", "Amm2", "down", "lo", "Amm1", "B40", "datt",
    "A10", "A40", "A50", "B50", "B10", "out", "Bmm1", "split", "heads0", "D30",
    "B00", "nat", "A30", "D40", "D50", "heads1", "A20", "A11", "B51", "A00",
    "D20", "B20", "D10", "D00", "B11", "B30", "A51", "A41", "free", "Qmm4",
    "Qmm5", "headb", "B52", "B01", "D31", "lastnorm", "B31", "Qmm0", "D41", "D51",
    "Qmm2", "Qmm3", "D21", "B41", "Qmm1", "D01", "A21", "A31", "v0", "D11",
    "Q40", "A01", "A42", "D02", "Q50", "v1", "Q00", "Q20", "Q10", "Q30",
    "B21", "D52", "Q41", "A12", "D32", "B02", "D22", "A22", "B32", "D12",
    "A43", "A02", "Q51", "v2", "B12", "A52", "B53", "D42", "Q21", "Q11",
    "A32", "Q31", "Q01", "B22", "B42", "D03", "Q42", "D13", "B03", "D23",
    "D43", "D53", "A53", "A13", "D33", "A23", "v3", "Q52", "B13", "Q22",
    "B33", "A03", "Q12", "A33", "Q32", "Q02", "B54", "B43", "B23", "D54",
    "Q43", "A44", "A14", "D14", "D34", "B14", "v4", "Q53", "Q23", "Q13",
    "A04", "D44", "Q33", "Q03", "D24", "D04", "A24", "B44", "A54", "B24",
    "B34", "A34", "B04", "Q24", "v5", "Q54", "Q14", "Q44", "Q34", "Q04",
    "Dfin", "Afin", "Qfin", "end",
)


def finish_down(place, down, d_acc, d_stage, d_in, f_send, f_recv, gdn_ref):
    for s in range(6):
        d_acc[pl.ds(48 * (s // 2), 48), pl.ds(128 * (s % 2), 128)] = down.last(s)
    for z in range(4):
        d_stage[z, pl.ds(0, 36), :] = d_acc[pl.ds(36 * z, 36), :]
        d_stage[z, pl.ds(36, 4), :] = jnp.zeros((4, 256), f32)
    targets = down_targets(place)
    swapped = place.x_hi != place.core
    moves = []
    for off in range(4):
        moves.append(
            push(
                place,
                d_stage.at[lax.rem(place.z + off, 4)],
                d_in.at[place.z],
                f_send.at[off],
                f_recv.at[off],
                targets[off],
            )
        )
    for off in range(1, 4):
        moves[off].start()

    @pl.when(swapped)
    def _():
        moves[0].start()
        moves[0].wait_recv()

    @pl.when(jnp.logical_not(swapped))
    def _():
        d_in[place.z] = d_stage[place.z]

    for off in range(1, 4):
        moves[off].wait_recv()
    for z in range(4):
        gdn_ref[:, pl.ds(256 * z, 256)] = d_in[z, pl.ds(0, 36), :]
    for off in range(1, 4):
        moves[off].wait_send()

    @pl.when(swapped)
    def _():
        moves[0].wait_send()


def lanes(rows):
    return lax.broadcasted_iota(jnp.int32, (rows, 128), 1)


def turn_heads(values):
    low = lax.rem(lanes(values.shape[0]), 64) < 32
    return jnp.where(low, pltpu.roll(values, 96, 1), pltpu.roll(values, 32, 1))


def head_mean(values):
    i = lax.broadcasted_iota(jnp.int32, (128, 128), 0)
    j = lax.broadcasted_iota(jnp.int32, (128, 128), 1)
    ones = jnp.where(lax.div(i, 64) == lax.div(j, 64), 1.0 / 64, 0.0).astype(bf16)
    high = values.astype(bf16)
    rest = (values - high.astype(f32)).astype(bf16)
    return dot(high, ones) + dot(rest, ones)


def gain_tiles(qk_gain):
    swapped = pltpu.roll(qk_gain, 64, 1)
    low = lax.broadcasted_iota(jnp.int32, (1, 128), 1) < 64
    return jnp.where(low, qk_gain, swapped), jnp.where(low, swapped, qk_gain)


def head_rows(values):
    low = lanes(values.shape[0]) < 64
    zero = jnp.zeros_like(values)
    return jnp.concatenate([jnp.where(low, values, zero), jnp.where(low, zero, values)], 0)


class Exchange:
    def __init__(self, place, out_at, into_at, send_sems, recv_sems):
        self.place = place
        self.out_at = out_at
        self.into_at = into_at
        self.send_sems = send_sems
        self.recv_sems = recv_sems

    def copy(self, m, off):
        j = lax.rem(self.place.ctx + off, 8)
        return push(
            self.place,
            self.out_at(m, j),
            self.into_at(m, self.place.ctx),
            self.send_sems.at[m, off - 1],
            self.recv_sems.at[m, off - 1],
            (self.place.rows, j),
        )

    def send(self, m):
        for off in range(1, 8):
            self.copy(m, off).start()
        self.into_at(m, self.place.ctx)[...] = self.out_at(m, self.place.ctx)[...]

    def arrived(self, m):
        for off in range(1, 8):
            self.copy(m, off).wait_recv()

    def sent(self):
        for m in range(2):
            for off in range(1, 8):
                self.copy(m, off).wait_send()


def ctx_peers(place):
    return [(place.rows, lax.rem(place.ctx + off, 8)) for off in range(1, 8)]


def document_edges(bounds_ref, m):
    index = lax.broadcasted_iota(jnp.int32, (1, 1024), 1)
    start = jnp.zeros((1, 1024), jnp.int32)
    end = jnp.full((1, 1024), 1024, jnp.int32)
    for k in range(1, 4):
        cut = bounds_ref[m, 0, k]
        start = jnp.where(index >= cut, cut, start)
        end = jnp.where(index < bounds_ref[m, 0, 4 - k], bounds_ref[m, 0, 4 - k], end)
    return start, end


def reorder_store(part, first, s, order, x_hi, at, width):
    part = part.reshape(4, 2, 8, 8, width)
    for y in range(4):
        for x_lo in range(2):
            for z in range(4):
                slot = slot_of(chip_number(x_hi, x_lo, y, z), order)
                first[s, slot, :, at] = part[y, :, 4 * x_lo + z].reshape(16, width).astype(bf16)


def block_kernel(
    bounds_ref,
    pos_ref,
    freq_ref,
    gain_ref,
    gain_ffn_ref,
    qk_gain_ref,
    x_hbm,
    cot_hbm,
    wgu_hbm,
    wd_hbm,
    w_qkv_hbm,
    w_out_hbm,
    out_hbm,
    gtok_hbm,
    ggu_ref,
    gdn_ref,
    gqkv_ref,
    gout_ref,
    vec_out,
    na_hbm,
    na_other_hbm,
    att_hbm,
    att_other_hbm,
    proj_hbm,
    qkv_hbm,
    o_hbm,
    a_first,
    a_held,
    b_first,
    b_held,
    d_first,
    d_held,
    nf,
    dyb,
    sum_send,
    sum_recv,
    mid_ref,
    dmid,
    cos_ref,
    sin_ref,
    l_ref,
    do_out,
    do_in,
    dpin,
    dmin,
    dm_own,
    g_fin,
    g_in,
    d_acc,
    d_stage,
    d_in,
    q_fin,
    q_in,
    vec,
    vec_in,
    w_sems,
    l_sems,
    x_send,
    x_recv,
    a_send,
    a_recv,
    b_send,
    b_recv,
    d_send,
    d_recv,
    q_send,
    q_recv,
    f_send,
    f_recv,
    k_send,
    k_recv,
    e_send,
    e_recv,
    do_send,
    do_recv,
    t_send,
    t_recv,
    v_send,
    v_recv,
    free_sem,
):
    place = Place()
    core = place.core
    partner = place.partner()
    every = slice(None)
    down = Scatter(place, DOWN_ORDERS, (d_first, every), (d_held, every), d_send, d_recv)
    gate = Scatter(place, GATE_ORDERS, (a_first, every), (a_held, every), a_send, a_recv)
    up = Scatter(place, UP_ORDERS, (b_first, every), (b_held, every), b_send, b_recv)
    narrow = pl.ds(0, 256)
    quad = Scatter(place, QUAD_ORDERS, (a_first, narrow), (b_first, narrow), q_send, q_recv)
    sums = {"D": down, "A": gate, "B": up, "Q": quad}
    steps = iter(STEPS)

    def run(ops, until):
        for name in steps:
            if name == until:
                return
            if name in ops:
                ops[name]()
            else:
                sums[name[0]].take(int(name[1]), int(name[2]))
    def t_at(m, j):
        return nf.at[
            pl.ds(pl.multiple_of(256 * m + 128 * lax.div(j, 4), 128), 128),
            pl.ds(pl.multiple_of(256 * lax.rem(j, 4), 256), 256),
        ]

    def tiles(ref, s, j, width):
        return ref.at[s, pl.ds(pl.multiple_of(8 * j, 8), 8), :, pl.ds(0, width)]

    heads_out = Exchange(
        place,
        lambda m, j: tiles(a_first, m, j, 256),
        lambda m, j: tiles(b_first, m, j, 256),
        k_send,
        k_recv,
    )
    heads_back = Exchange(
        place,
        lambda m, j: tiles(b_first, 4 + m, j, 128),
        lambda m, j: tiles(b_first, 2 + m, j, 128),
        e_send,
        e_recv,
    )
    grads_out = Exchange(
        place, lambda m, j: do_out.at[m, j], lambda m, j: do_in.at[m, j], do_send, do_recv
    )
    own_rows = pl.ds(0, 256)
    other_rows = pl.ds(256, 256)
    to_dy = push(place, cot_hbm, dyb.at[other_rows], x_send.at[0], x_recv.at[0], partner)
    to_nf = push(place, nf.at[own_rows], nf.at[other_rows], x_send.at[1], x_recv.at[1], partner)
    to_out = push(place, sum_send, sum_recv.at[0], x_send.at[2], x_recv.at[2], partner)
    to_back = push(place, sum_send, sum_recv.at[1], x_send.at[3], x_recv.at[3], partner)
    to_att = push(place, dm_own, att_other_hbm, x_send.at[5], x_recv.at[5], partner)
    att_copy = pltpu.make_async_copy(dm_own, att_hbm, l_sems.at[7])
    qkv_copy = pltpu.make_async_copy(
        b_first.at[pl.ds(0, 2), :, :, pl.ds(0, 256)], qkv_hbm, l_sems.at[8]
    )
    o_copy = pltpu.make_async_copy(
        b_first.at[pl.ds(4, 2), :, :, pl.ds(0, 128)], o_hbm, l_sems.at[9]
    )
    cot_load = pltpu.make_async_copy(cot_hbm, dyb.at[own_rows], l_sems.at[1])
    low = lanes(256) < 64
    gain_q, gain_k = gain_tiles(qk_gain_ref[...])

    def attend(w_qkv, x_ref, na, proj_ref, q2, kk, vo):
        x_load = pltpu.make_async_copy(x_hbm, x_ref, l_sems.at[2])
        w_load = pltpu.make_async_copy(w_qkv_hbm, w_qkv, l_sems.at[3])
        na_copy = pltpu.make_async_copy(na, na_hbm, l_sems.at[4])
        proj_copy = pltpu.make_async_copy(proj_ref, proj_hbm, l_sems.at[5])
        for load in (x_load, w_load, cot_load):
            load.start()
        greet_all(
            place,
            [partner] + [place.neighbour(dim) for dim in range(6)] + ctx_peers(place),
        )
        to_dy.start()
        columns = jnp.concatenate(
            [pos_ref[0].astype(f32), pos_ref[1].astype(f32), jnp.zeros((6, 128), f32)], 0
        ).T
        sign = jnp.where(lax.rem(lanes(128), 64) < 32, -1.0, 1.0)
        for m in range(2):
            angle = columns[:, m : m + 1] * freq_ref[...]
            cos_ref[pl.ds(128 * m, 128), :] = jnp.cos(angle)
            sin_ref[pl.ds(128 * m, 128), :] = jnp.sin(angle) * sign
        x_load.wait()
        inputs = x_ref[...].astype(f32)
        scale = lax.rsqrt(jnp.mean(inputs * inputs, axis=-1, keepdims=True) + norm_eps)
        na[...] = (inputs * scale * gain_ref[...]).astype(bf16)
        to_na = push(place, na, na_other_hbm, x_send.at[4], x_recv.at[4], partner)
        na_copy.start()
        w_load.wait()

        def turned(tile, gain):
            u = tile * lax.rsqrt(head_mean(tile * tile) + norm_eps) * gain
            return u * cos_ref[...] + turn_heads(u) * sin_ref[...]

        def store(at, j, tile):
            for m in range(2):
                rows = tile[128 * m : 128 * m + 128].astype(bf16)
                a_first[m, pl.ds(8 * j, 8), :, pl.ds(at, 128)] = rows.reshape(8, 16, 128)

        for i in range(4):
            pair = dot(na[...], w_qkv[:, pl.ds(256 * i, 256)])
            proj_ref[:, pl.ds(256 * i, 256)] = pair
            for j in range(2):
                store(0, 2 * i + j, turned(pair[:, 128 * j : 128 * j + 128], gain_q) * 0.125)
        for i in range(2):
            key_pair = dot(na[...], w_qkv[:, pl.ds(1024 + 256 * i, 256)])
            value_pair = dot(na[...], w_qkv[:, pl.ds(1536 + 256 * i, 256)])
            proj_ref[:, pl.ds(1024 + 256 * i, 256)] = key_pair
            for j in range(2):
                key = turned(key_pair[:, 128 * j : 128 * j + 128], gain_k)
                value = value_pair[:, 128 * j : 128 * j + 128]
                store(128, 4 * i + 2 * j, jnp.where(low, key, pltpu.roll(value, 64, 1)))
                store(128, 4 * i + 2 * j + 1, jnp.where(low, pltpu.roll(key, 64, 1), value))
        for m in range(2):
            heads_out.send(m)
        to_na.start()
        proj_copy.start()

        def heads(m, carry):
            heads_out.arrived(m)
            ends = document_edges(bounds_ref, m)[1]
            for b in range(4):
                query = b_first[m, pl.ds(16 * b, 16), :, pl.ds(0, 128)].reshape(256, 128)
                pair = b_first[m, pl.ds(16 * b, 16), :, pl.ds(128, 128)].reshape(256, 128)
                pair = pair.astype(f32)
                swapped = pltpu.roll(pair, 64, 1)
                q2[b] = head_rows(query)
                kk[b] = jnp.where(low, pair, swapped).astype(bf16)
                vo[b] = jnp.where(low, swapped, 1.0).astype(bf16)
            for qb in range(4):
                acc = jnp.zeros((512, 128), f32)
                for kb in range(qb + 1):
                    scores = dot_cols(q2[qb], kk[kb])
                    t = 256 * qb + lax.rem(lax.broadcasted_iota(jnp.int32, (512, 256), 0), 256)
                    keep = t < ends[:, 256 * kb : 256 * kb + 256]
                    if kb == qb:
                        s = 256 * kb + lax.broadcasted_iota(jnp.int32, (512, 256), 1)
                        keep = keep & (s <= t)
                    weights = jnp.where(keep, jnp.exp(scores), 0.0).astype(bf16)
                    acc = acc + dot(weights, vo[kb])
                total = pltpu.roll(acc, 64, 1)
                head0 = acc[:256]
                head1 = pltpu.roll(acc[256:], 64, 1)
                denominator = jnp.where(low, total[:256], acc[256:])
                out = jnp.where(low, head0, head1) / denominator
                log_total = jnp.log(denominator).T
                l_ref[m, pl.ds(0, 1), pl.ds(256 * qb, 256)] = log_total[0:1]
                l_ref[m, pl.ds(1, 1), pl.ds(256 * qb, 256)] = log_total[64:65]
                b_first[4 + m, pl.ds(16 * qb, 16), :, pl.ds(0, 128)] = out.astype(bf16).reshape(
                    16, 16, 128
                )
            heads_back.send(m)
            return carry

        lax.fori_loop(0, 2, heads, 0)
        qkv_copy.start()
        o_copy.start()
        na_copy.wait()
        proj_copy.wait()
        to_na.wait()

    pl.run_scoped(
        attend,
        pltpu.VMEM((1024, 2048), bf16),
        pltpu.VMEM((256, 1024), bf16),
        pltpu.VMEM((256, 1024), bf16),
        pltpu.VMEM((256, 1536), f32),
        pltpu.VMEM((4, 512, 128), bf16),
        pltpu.VMEM((4, 256, 128), bf16),
        pltpu.VMEM((4, 256, 128), bf16),
    )

    to_dm = push(place, dm_own.at[1 - core], dmin, x_send.at[6], x_recv.at[6], partner)
    out_copy = pltpu.make_async_copy(sum_send, out_hbm, l_sems.at[0])

    def feed_forward(wgu, wd, nft, h, ht, dgu, sum_own):
        def unit_loads(i):
            at = pl.multiple_of(core * FF_HALF + 768 * i, 256)
            up_at = pl.multiple_of(4608 + core * FF_HALF + 768 * i, 256)
            here = pl.ds(pl.multiple_of(768 * i, 256), 768)
            up_here = pl.ds(pl.multiple_of(FF_HALF + 768 * i, 256), 768)
            return [
                pltpu.make_async_copy(
                    wgu_hbm.at[:, pl.ds(at, 768)], wgu.at[:, here], w_sems.at[3 * i]
                ),
                pltpu.make_async_copy(
                    wgu_hbm.at[:, pl.ds(up_at, 768)], wgu.at[:, up_here], w_sems.at[3 * i + 1]
                ),
                pltpu.make_async_copy(
                    wd_hbm.at[pl.ds(at, 768)], wd.at[here], w_sems.at[3 * i + 2]
                ),
            ]

        w_out_loads = [
            pltpu.make_async_copy(
                w_out_hbm.at[pl.ds(512 * i, 512)], dgu.at[:, pl.ds(1024 * i, 1024)], l_sems.at[2 + i]
            )
            for i in range(2)
        ]
        x_load = pltpu.make_async_copy(x_hbm, sum_send, l_sems.at[4])
        for load in (x_load, *w_out_loads):
            load.start()
        for i in range(3):
            for copy in unit_loads(i):
                copy.start()
        for m in range(2):
            heads_back.arrived(m)
            for j in range(8):
                tile = b_first[2 + m, pl.ds(8 * j, 8), :, pl.ds(0, 128)].reshape(128, 128)
                dm_own[j // 4, pl.ds(128 * m, 128), pl.ds(128 * (j % 4), 128)] = tile
        to_att.start()
        att_copy.start()
        for load in (x_load, *w_out_loads):
            load.wait()
        mid = sum_send[...].astype(f32) + (
            dot(dm_own[0], dgu[:, pl.ds(0, 1024)]) + dot(dm_own[1], dgu[:, pl.ds(1024, 1024)])
        )
        mid_ref[...] = mid
        scale = lax.rsqrt(jnp.mean(mid * mid, axis=-1, keepdims=True) + norm_eps)
        nf[own_rows, :] = (mid * scale * gain_ffn_ref[...]).astype(bf16)
        to_nf.start()
        nft[:, own_rows] = nf[own_rows, :].T
        heads_out.sent()
        heads_back.sent()
        qkv_copy.wait()
        o_copy.wait()
        cot_load.wait()
        to_dy.wait_recv()
        to_nf.wait_recv()
        nft[:, other_rows] = nf[other_rows, :].T

        def units(i, carry):
            @pl.when(lax.rem(i, 3) == 0)
            def _():
                for copy in unit_loads(lax.div(i, 3)):
                    copy.wait()

            cols = pl.ds(pl.multiple_of(256 * i, 256), 256)
            up_cols = pl.ds(pl.multiple_of(FF_HALF + 256 * i, 256), 256)
            gated = dot(nf[...], wgu[:, cols])
            upward = dot(nf[...], wgu[:, up_cols])
            grad_hidden = dot_cols(dyb[...], wd[cols, :])
            sigma = 1.0 / (1.0 + jnp.exp(-gated))
            silu = gated * sigma
            h[:, cols] = (silu * upward).astype(bf16)
            dgu[:, cols] = (grad_hidden * upward * (sigma + silu * (1.0 - sigma))).astype(bf16)
            dgu[:, up_cols] = (grad_hidden * silu).astype(bf16)
            return carry

        lax.fori_loop(0, 9, units, 0)

        def down_grads():
            for block in range(3):
                ht[...] = h[:, pl.ds(768 * block, 768)].T
                for z in range(4):
                    part = dot(ht[...], dyb[:, pl.ds(256 * z, 256)])
                    for i in range(16):
                        q = 16 * block + i
                        y, core_to, x_lo, rg = q // 12, (q // 6) % 2, (q // 3) % 2, q % 3
                        for ch in range(2):
                            s = 2 * rg + ch
                            slot = slot_of(chip_number(core_to, x_lo, y, z), DOWN_ORDERS[s])
                            d_first[s, slot] = part[
                                48 * i : 48 * i + 48, 128 * ch : 128 * ch + 128
                            ].astype(bf16)
            for s in range(6):
                down.send(s, 0)

        def back_to_norm():
            def pair(i, carry):
                for j in range(2):
                    at = pl.ds(pl.multiple_of(512 * i + 256 * j, 256), 256)
                    part = dot_cols(dgu[...], wgu[at, :])
                    dmid[:, at] = part[:256]
                    sum_send[:, at] = part[256:].astype(bf16)
                return carry

            lax.fori_loop(0, 2, pair, 0)
            to_back.start()

        def wide_grads(scatter, first, base, orders, p):
            for x_hi in range(2):
                rows = nft[pl.ds(512 * x_hi, 512), :]
                for j in range(3):
                    part = dot(rows, dgu[:, pl.ds(base + 768 * p + 256 * j, 256)])
                    for k in range(2):
                        tile = 2 * j + k
                        s = 2 * p + tile // 3
                        reorder_store(
                            part[:, 128 * k : 128 * k + 128],
                            first,
                            s,
                            orders[s],
                            x_hi,
                            pl.ds(128 * (tile % 3), 128),
                            128,
                        )
            for s in (2 * p, 2 * p + 1):
                scatter.send(s, 0)

        w_out_load = pltpu.make_async_copy(w_out_hbm, wd.at[pl.ds(0, 1024)], l_sems.at[4])

        def output():
            to_back.wait_send()

            def pair(i, carry):
                for j in range(2):
                    at = pl.ds(pl.multiple_of(512 * i + 256 * j, 256), 256)
                    part = dot(h[...], wd[:, at])
                    sum_own[:, at] = part[:256]
                    sum_send[:, at] = part[256:].astype(bf16)
                return carry

            lax.fori_loop(0, 2, pair, 0)
            to_out.start()
            w_out_load.start()

        def output_sum():
            to_out.wait()
            sum_send[...] = (mid_ref[...] + sum_own[...] + sum_recv[0].astype(f32)).astype(bf16)
            out_copy.start()

        def norm_back():
            to_back.wait_recv()
            mid = mid_ref[...]
            scale = lax.rsqrt(jnp.mean(mid * mid, axis=-1, keepdims=True) + norm_eps)
            normed = mid * scale
            grad_nffn = dmid[...] + sum_recv[1].astype(f32)
            gain_grad = jnp.sum(grad_nffn * normed, axis=0, keepdims=True)
            for i in range(8):
                vec[0, pl.ds(8 + i, 1), :] = gain_grad[:, 128 * i : 128 * i + 128]
            grad_e = grad_nffn * gain_ffn_ref[...]
            dmid[...] = dyb[own_rows, :].astype(f32) + scale * (
                grad_e - normed * jnp.mean(grad_e * normed, axis=-1, keepdims=True)
            )
            to_att.wait_send()
            att_copy.wait()
            for half in range(2):
                dm_own[half] = dmid[:, pl.ds(512 * half, 512)].astype(bf16)
            to_dm.start()

            to_nf.wait_send()
            w_out_load.wait()
            for i in range(4):
                pair = dot_cols(dm_own[0], wd[pl.ds(256 * i, 256), pl.ds(0, 512)]) + dot_cols(
                    dm_own[1], wd[pl.ds(256 * i, 256), pl.ds(512, 512)]
                )
                for j in range(2):
                    for m in range(2):
                        do_out[m, 2 * i + j] = pair[
                            128 * m : 128 * m + 128, 128 * j : 128 * j + 128
                        ].astype(bf16)
            for m in range(2):
                grads_out.send(m)

        ops = {
            "down": down_grads,
            "dn": back_to_norm,
            "lo": output,
            "datt": norm_back,
            "out": output_sum,
        }
        for p in range(3):
            ops[f"Amm{p}"] = functools.partial(wide_grads, gate, a_first, 0, GATE_ORDERS, p)
            ops[f"Bmm{p}"] = functools.partial(wide_grads, up, b_first, FF_HALF, UP_ORDERS, p)
        run(ops, "split")

    pl.run_scoped(
        feed_forward,
        pltpu.VMEM((1024, 4608), bf16),
        pltpu.VMEM((FF_HALF, 1024), bf16),
        pltpu.VMEM((1024, 512), bf16),
        pltpu.VMEM((512, FF_HALF), bf16),
        pltpu.VMEM((768, 512), bf16),
        pltpu.VMEM((512, 4608), bf16),
        pltpu.VMEM((256, 1024), f32),
    )

    def vec_move(step):
        device = place.neighbour(step) if step < 6 else partner
        return push(place, vec.at[step], vec_in.at[step], v_send.at[step], v_recv.at[step], device)

    def vec_take(step):
        vec_move(step).wait_recv()
        vec[step + 1] = vec[step] + vec_in[step]
        vec_move(step + 1).start()

    def down_end():
        finish_down(place, down, d_acc, d_stage, d_in, f_send, f_recv, gdn_ref)

    swap = push(place, g_fin.at[1 - core], g_in, x_send.at[8], x_recv.at[8], partner)
    swap_q = push(place, q_fin.at[1 - core], q_in, x_send.at[9], x_recv.at[9], partner)

    def wide_end():
        for s in range(12):
            total = (gate if s < 6 else up).last(s % 6)
            g_fin[0, s] = total[:8]
            g_fin[1, s] = total[8:]
        swap.start()

    def quad_end():
        for s in range(6):
            total = quad.last(s)
            q_fin[0, s] = total[:8]
            q_fin[1, s] = total[8:]
        swap_q.start()

    def attention_back(
        w_qkv, x_ref, gtok, proj_ref, qkv_ref, o_ref, q2, do2, kk, vv, kt, delta, dq, dp,
        na_own, na_other, att_own, att_other, nat, attt, cols, t_out,
    ):
        sources = [qkv_hbm, o_hbm, proj_hbm, x_hbm, w_qkv_hbm]
        loads = [
            pltpu.make_async_copy(source, target, w_sems.at[i])
            for i, (source, target) in enumerate(
                zip(sources, [qkv_ref, o_ref, proj_ref, x_ref, w_qkv], strict=True)
            )
        ]
        for load in loads:
            load.start()
        grads_back = Exchange(place, lambda m, j: t_out.at[m, j], t_at, t_send, t_recv)

        def heads_grad(m):
            if m == 0:
                for load in loads[:2]:
                    load.wait()
            grads_out.arrived(m)
            starts = document_edges(bounds_ref, m)[0]
            for b in range(4):
                query = qkv_ref[m, pl.ds(16 * b, 16), :, pl.ds(0, 128)].reshape(256, 128)
                pair = qkv_ref[m, pl.ds(16 * b, 16), :, pl.ds(128, 128)].reshape(256, 128)
                pair = pair.astype(f32)
                grad = do_in[m, pl.ds(2 * b, 2)].reshape(256, 128)
                swapped = pltpu.roll(pair, 64, 1)
                key_pair = jnp.where(low, pair, swapped)
                q2[b] = head_rows(query)
                do2[b] = head_rows(grad)
                kk[b] = key_pair.astype(bf16)
                vv[b] = jnp.where(low, swapped, pair).astype(bf16)
                kt[b] = key_pair.T.astype(bf16)
                out = o_ref[m, pl.ds(16 * b, 16)].reshape(256, 128).astype(f32)
                inner = (grad.astype(f32) * out).T
                delta[b, :, pl.ds(0, 256)] = jnp.sum(inner[:64], axis=0, keepdims=True)
                delta[b, :, pl.ds(256, 256)] = jnp.sum(inner[64:], axis=0, keepdims=True)
            for kb in range(4):
                grad_key = jnp.zeros((256, 128), f32)
                grad_value = jnp.zeros((256, 128), f32)
                for qb in range(kb, 4):
                    scores = dot_cols(kk[kb], q2[qb])
                    log_total = jnp.concatenate(
                        [l_ref[m, pl.ds(i, 1), pl.ds(256 * qb, 256)] for i in range(2)], 1
                    )
                    start = starts[:, 256 * qb : 256 * qb + 256]
                    s = 256 * kb + lax.broadcasted_iota(jnp.int32, (256, 512), 0)
                    keep = s >= jnp.concatenate([start, start], 1)
                    if kb == qb:
                        t = lax.broadcasted_iota(jnp.int32, (256, 512), 1)
                        keep = keep & (s <= 256 * qb + lax.rem(t, 256))
                    probs = jnp.where(keep, jnp.exp(scores - log_total), 0.0)
                    grad_probs = dot_cols(vv[kb], do2[qb])
                    grad_scores = (probs * (grad_probs - delta[qb])).astype(bf16)
                    grad_value = grad_value + dot(probs.astype(bf16), do2[qb])
                    grad_key = grad_key + dot(grad_scores, q2[qb])
                    grad_query = dot(kt[kb], grad_scores)
                    if kb == 0:
                        dq[qb] = grad_query[:64]
                    else:
                        dq[qb] = dq[qb] + grad_query[:64]
                grad_key = grad_key + pltpu.roll(grad_key, 64, 1)
                grad_value = grad_value + pltpu.roll(grad_value, 64, 1)
                tile = jnp.where(low, grad_key, grad_value).astype(bf16)
                for half in range(2):
                    rows = slice(128 * half, 128 * half + 128)
                    t_out[m, 2 * kb + half, :, pl.ds(128, 128)] = tile[rows]
            for qb in range(4):
                stacked = jnp.concatenate([dq[qb, :, pl.ds(0, 256)], dq[qb, :, pl.ds(256, 256)]], 0)
                tile = (stacked * 0.125).T.astype(bf16)
                for half in range(2):
                    rows = slice(128 * half, 128 * half + 128)
                    t_out[m, 2 * qb + half, :, pl.ds(0, 128)] = tile[rows]
            grads_back.send(m)

        def sums_free():
            gate.sent([0])
            up.sent([0])
            for dim in range(6):
                pl.semaphore_signal(
                    free_sem, inc=1, device_id=place.neighbour(dim), device_id_type=MESH
                )

        sides = [
            pltpu.make_async_copy(source, target, l_sems.at[2 + i])
            for i, (source, target) in enumerate(
                zip(
                    [na_hbm, att_hbm, na_other_hbm, att_other_hbm],
                    [na_own, att_own, na_other, att_other],
                    strict=True,
                )
            )
        ]
        for load in sides[:3]:
            load.start()

        def token_sides():
            to_att.wait_recv()
            sides[3].start()
            for load in sides[:3]:
                load.wait()
            nat[:, own_rows] = na_own[...].T
            nat[:, other_rows] = na_other[...].T
            sides[3].wait()
            for i in range(2):
                attt[pl.ds(512 * i, 512), own_rows] = att_own[i].T
                attt[pl.ds(512 * i, 512), other_rows] = att_other[i].T
            to_dm.wait_recv()
            cols[own_rows, pl.ds(1024, 512)] = dm_own[core]
            cols[other_rows, pl.ds(1024, 512)] = dmin[...]

        def projection_grads(s):
            left = nat if s < 4 else attt
            if s == 0:
                to_dp.wait_recv()
                cols[other_rows, pl.ds(0, 1024)] = dpin[...]
            for x_hi in range(2):
                part = dot(left[pl.ds(512 * x_hi, 512), :], cols[:, pl.ds(256 * s, 256)])
                reorder_store(part, a_first, s, QUAD_ORDERS[s], x_hi, narrow, 256)
            if s == 4:
                pl.semaphore_wait(free_sem, 6)
            quad.send(s, 0)

        def both_rows(j, at):
            return jnp.concatenate([t_at(m, j)[:, pl.ds(at, 128)] for m in range(2)], 0).astype(f32)

        def head_back(grad, value, gain):
            grad = grad * cos_ref[...] + turn_heads(grad * sin_ref[...])
            scale = lax.rsqrt(head_mean(value * value) + norm_eps)
            normed = value * scale
            grad_e = grad * gain
            gain_grad = jnp.sum(grad * normed, axis=0, keepdims=True)
            return scale * (grad_e - normed * head_mean(grad_e * normed)), gain_grad

        to_dp = push(place, dp.at[1 - core], dpin, x_send.at[7], x_recv.at[7], partner)
        gtok_copy = pltpu.make_async_copy(gtok, gtok_hbm, l_sems.at[1])

        def turn_back():
            loads[2].wait()
            for m in range(2):
                grads_back.arrived(m)
            sum_k = jnp.zeros((1, 128), f32)

            def query_pair(i, total):
                for j in range(2):
                    at = pl.ds(pl.multiple_of(256 * i + 128 * j, 128), 128)
                    back, part = head_back(both_rows(2 * i + j, 0), proj_ref[:, at], gain_q)
                    dp[0, :, at] = back.astype(bf16)
                    total = total + part
                return total

            sum_q = lax.fori_loop(0, 4, query_pair, jnp.zeros((1, 128), f32))
            for i in range(4):
                first = both_rows(2 * i, 128)
                second = both_rows(2 * i + 1, 128)
                grad_key = jnp.where(low, first, pltpu.roll(second, 64, 1))
                grad_value = jnp.where(low, pltpu.roll(first, 64, 1), second)
                back, part = head_back(grad_key, proj_ref[:, pl.ds(1024 + 128 * i, 128)], gain_k)
                dp[1, :, pl.ds(128 * i, 128)] = back.astype(bf16)
                dp[1, :, pl.ds(512 + 128 * i, 128)] = grad_value.astype(bf16)
                sum_k = sum_k + part
            to_dp.start()
            sum_q = sum_q + pltpu.roll(sum_q, 64, 1)
            sum_k = sum_k + pltpu.roll(sum_k, 64, 1)
            vec[0, pl.ds(16, 8), :] = jnp.zeros((8, 128), f32)
            vec[0, pl.ds(16, 1), :] = jnp.where(
                lax.broadcasted_iota(jnp.int32, (1, 128), 1) < 64, sum_q, sum_k
            )
            cols[own_rows, pl.ds(0, 1024)] = dp[core]

        def last_norm():
            loads[3].wait()
            loads[4].wait()
            inputs = x_ref[...].astype(f32)
            scale = lax.rsqrt(jnp.mean(inputs * inputs, axis=-1, keepdims=True) + norm_eps)
            normed = inputs * scale
            grad_n = dot_cols(dp[0], w_qkv[:, pl.ds(0, 1024)]) + dot_cols(
                dp[1], w_qkv[:, pl.ds(1024, 1024)]
            )
            gain_grad = jnp.sum(grad_n * normed, axis=0, keepdims=True)
            grad_e = grad_n * gain_ref[...]
            gtok[...] = dmid[...] + scale * (
                grad_e - normed * jnp.mean(grad_e * normed, axis=-1, keepdims=True)
            )
            gtok_copy.start()
            for i in range(8):
                vec[0, pl.ds(i, 1), :] = gain_grad[:, 128 * i : 128 * i + 128]
            vec_move(0).start()

        ops = {
            "heads0": functools.partial(heads_grad, 0),
            "heads1": functools.partial(heads_grad, 1),
            "free": sums_free,
            "nat": token_sides,
            "headb": turn_back,
            "lastnorm": last_norm,
            "Dfin": down_end,
            "Afin": wide_end,
            "Qfin": quad_end,
        }
        for s in range(6):
            ops[f"Qmm{s}"] = functools.partial(projection_grads, s)
            ops[f"v{s}"] = functools.partial(vec_take, s)
        run(ops, "end")
        gtok_copy.wait()
        to_dp.wait_send()
        grads_back.sent()

    pl.run_scoped(
        attention_back,
        pltpu.VMEM((1024, 2048), bf16),
        pltpu.VMEM((256, 1024), bf16),
        pltpu.VMEM((256, 1024), f32),
        pltpu.VMEM((256, 1536), f32),
        pltpu.VMEM((2, 64, 16, 256), bf16),
        pltpu.VMEM((2, 64, 16, 128), bf16),
        pltpu.VMEM((4, 512, 128), bf16),
        pltpu.VMEM((4, 512, 128), bf16),
        pltpu.VMEM((4, 256, 128), bf16),
        pltpu.VMEM((4, 256, 128), bf16),
        pltpu.VMEM((4, 128, 256), bf16),
        pltpu.VMEM((4, 1, 512), f32),
        pltpu.VMEM((4, 64, 512), f32),
        pltpu.VMEM((2, 256, 1024), bf16),
        pltpu.VMEM((256, 1024), bf16),
        pltpu.VMEM((256, 1024), bf16),
        pltpu.VMEM((2, 256, 512), bf16),
        pltpu.VMEM((2, 256, 512), bf16),
        pltpu.VMEM((1024, 512), bf16),
        pltpu.VMEM((1024, 512), bf16),
        pltpu.VMEM((512, 1536), bf16),
        pltpu.VMEM((2, 8, 128, 256), bf16),
    )

    def wide_cols(of, s):
        return pl.ds(pl.multiple_of((s // 6) * 4608 + of * FF_HALF + (s % 6) * 384, 128), 384)

    def quad_cols(of, s):
        if s < 4:
            return gqkv_ref, pl.ds(pl.multiple_of(of * 1024 + 256 * s, 256), 256)
        return gout_ref, pl.ds(pl.multiple_of(of * 512 + 256 * (s - 4), 256), 256)

    for s in range(12):
        ggu_ref[:, wide_cols(core, s)] = g_fin[core, s]
    swap.wait_recv()
    for s in range(12):
        ggu_ref[:, wide_cols(1 - core, s)] = g_in[s]
    for s in range(6):
        ref, at = quad_cols(core, s)
        ref[:, at] = q_fin[core, s]
    swap_q.wait_recv()
    for s in range(6):
        ref, at = quad_cols(1 - core, s)
        ref[:, at] = q_in[s]
    vec_move(6).wait_recv()
    vec_out[...] = vec[6] + vec_in[6]

    for move in (to_dy, to_dm, swap, swap_q):
        move.wait_send()
    out_copy.wait()
    for step in range(7):
        vec_move(step).wait_send()
    down.sent()
    gate.sent(range(1, 6))
    up.sent(range(1, 6))
    quad.sent()
    grads_out.sent()


def block(bounds, *arrays):
    vmem = pl.BlockSpec(memory_space=pltpu.VMEM)
    hbm = pl.BlockSpec(memory_space=pl.ANY)
    smem = pl.BlockSpec(memory_space=pltpu.SMEM)
    dma = pltpu.SemaphoreType.DMA
    return pl.pallas_call(
        block_kernel,
        out_shape=(
            jax.ShapeDtypeStruct((256, 1024), bf16),
            jax.ShapeDtypeStruct((256, 1024), f32),
            jax.ShapeDtypeStruct((8, 9216), f32),
            jax.ShapeDtypeStruct((36, 1024), f32),
            jax.ShapeDtypeStruct((8, 2048), f32),
            jax.ShapeDtypeStruct((8, 1024), f32),
            jax.ShapeDtypeStruct((24, 128), f32),
            jax.ShapeDtypeStruct((256, 1024), bf16),
            jax.ShapeDtypeStruct((256, 1024), bf16),
            jax.ShapeDtypeStruct((2, 256, 512), bf16),
            jax.ShapeDtypeStruct((2, 256, 512), bf16),
            jax.ShapeDtypeStruct((256, 1536), f32),
            jax.ShapeDtypeStruct((2, 64, 16, 256), bf16),
            jax.ShapeDtypeStruct((2, 64, 16, 128), bf16),
        ),
        in_specs=[smem] + [vmem] * 5 + [hbm] * 6,
        out_specs=(hbm, hbm) + (vmem,) * 5 + (hbm,) * 7,
        scratch_shapes=[
            pltpu.VMEM((6, 64, 16, 384), bf16),
            pltpu.VMEM((6, 63, 16, 384), bf16),
            pltpu.VMEM((6, 64, 16, 384), bf16),
            pltpu.VMEM((6, 63, 16, 384), bf16),
            pltpu.VMEM((6, 64, 48, 128), bf16),
            pltpu.VMEM((6, 63, 48, 128), bf16),
            pltpu.VMEM((512, 1024), bf16),
            pltpu.VMEM((512, 1024), bf16),
            pltpu.VMEM((256, 1024), bf16),
            pltpu.VMEM((2, 256, 1024), bf16),
            pltpu.VMEM((256, 1024), f32),
            pltpu.VMEM((256, 1024), f32),
            pltpu.VMEM((256, 128), f32),
            pltpu.VMEM((256, 128), f32),
            pltpu.VMEM((2, 2, 1024), f32),
            pltpu.VMEM((2, 8, 128, 128), bf16),
            pltpu.VMEM((2, 8, 128, 128), bf16),
            pltpu.VMEM((256, 1024), bf16),
            pltpu.VMEM((256, 512), bf16),
            pltpu.VMEM((2, 256, 512), bf16),
            pltpu.VMEM((2, 12, 8, 384), f32),
            pltpu.VMEM((12, 8, 384), f32),
            pltpu.VMEM((144, 256), f32),
            pltpu.VMEM((4, 40, 256), f32),
            pltpu.VMEM((4, 40, 256), f32),
            pltpu.VMEM((2, 6, 8, 256), f32),
            pltpu.VMEM((6, 8, 256), f32),
            pltpu.VMEM((7, 24, 128), f32),
            pltpu.VMEM((7, 24, 128), f32),
            dma((9,)),
            dma((10,)),
            dma((10,)),
            dma((10,)),
            dma((6, 6)),
            dma((6, 6)),
            dma((6, 6)),
            dma((6, 6)),
            dma((6, 6)),
            dma((6, 6)),
            dma((6, 6)),
            dma((6, 6)),
            dma((4,)),
            dma((4,)),
            dma((2, 7)),
            dma((2, 7)),
            dma((2, 7)),
            dma((2, 7)),
            dma((2, 7)),
            dma((2, 7)),
            dma((2, 7)),
            dma((2, 7)),
            dma((7,)),
            dma((7,)),
            pltpu.SemaphoreType.REGULAR,
        ],
        compiler_params=pltpu.CompilerParams(
            collective_id=0, has_side_effects=True, vmem_limit_bytes=VMEM_LIMIT
        ),
        name="transformer_block",
    )(bounds, *arrays)


def finish_kernel(*refs):
    arrays, vec = refs[:6], refs[6]
    targets, (gain_a, gain_f, gain_qk) = refs[7:13], refs[13:16]
    passing, (in_sems, out_sems) = refs[16:22], refs[22:]
    reads = [
        pltpu.make_async_copy(array, held, in_sems.at[i])
        for i, (array, held) in enumerate(zip(arrays, passing, strict=True))
    ]
    writes = [
        pltpu.make_async_copy(held, target, out_sems.at[i])
        for i, (held, target) in enumerate(zip(passing, targets, strict=True))
    ]
    for read in reads:
        read.start()
    own = lax.axis_index("rows") * 8 + lax.axis_index("ctx")
    row = lax.div(own, 16)
    at = lax.rem(own, 16)
    lane = lax.broadcasted_iota(jnp.int32, (8, 128), 1)
    tile = lax.broadcasted_iota(jnp.int32, (8, 128), 0)

    def pick(values, of_row, of_lane, count):
        kept = jnp.sum(jnp.where(tile == of_row, values, 0.0), axis=0, keepdims=True)
        place = lax.broadcasted_iota(jnp.int32, (128, count), 0)
        order = lax.broadcasted_iota(jnp.int32, (128, count), 1)
        rows = jnp.broadcast_to(kept, (8, 128)).T[:, :count]
        return jnp.sum(jnp.where(place == of_lane + order, rows, 0.0), axis=0, keepdims=True)

    gain_a[...] = pick(vec[pl.ds(0, 8), :], row, 8 * at, 8)
    gain_f[...] = pick(vec[pl.ds(8, 8), :], row, 8 * at, 8)
    gain_qk[...] = pick(vec[pl.ds(16, 8), :], 0, own, 1)
    for read, write in zip(reads, writes, strict=True):
        read.wait()
        write.start()
    for write in writes:
        write.wait()


def finish(out, gtok, ggu, gdn, gqkv, gout, vec):
    vmem = pl.BlockSpec(memory_space=pltpu.VMEM)
    hbm = pl.BlockSpec(memory_space=pl.ANY)
    same = [jax.ShapeDtypeStruct(a.shape, a.dtype) for a in (out, gtok, ggu, gdn, gqkv, gout)]
    return pl.pallas_call(
        finish_kernel,
        out_shape=(
            *same,
            jax.ShapeDtypeStruct((1, 8), f32),
            jax.ShapeDtypeStruct((1, 8), f32),
            jax.ShapeDtypeStruct((1, 1), f32),
        ),
        in_specs=[hbm] * 6 + [vmem],
        out_specs=(hbm,) * 6 + (vmem,) * 3,
        scratch_shapes=[pltpu.VMEM(a.shape, a.dtype) for a in same]
        + [pltpu.SemaphoreType.DMA((6,)), pltpu.SemaphoreType.DMA((6,))],
        name="results",
    )(out, gtok, ggu, gdn, gqkv, gout, vec)


def local(
    tokens,
    cotangent,
    bounds,
    positions,
    norm_gain_attn,
    w_qkv,
    qk_gain,
    w_out,
    norm_gain_ffn,
    w_gate_up,
    w_down,
):
    lane = np.arange(128) % 32
    freqs = (rope_theta ** (-2.0 * lane / 64)).astype(np.float32)[None]
    results = block(
        bounds,
        positions,
        freqs,
        norm_gain_attn[None],
        norm_gain_ffn[None],
        qk_gain[None],
        tokens.reshape(256, 1024),
        cotangent.reshape(256, 1024),
        w_gate_up,
        w_down,
        w_qkv,
        w_out,
    )
    layer_out, grad_tokens, sum_gate_up, sum_down, sum_qkv, sum_out, gain_a, gain_f, gain_qk = (
        finish(*results[:7])
    )
    return (
        layer_out.reshape(tokens.shape),
        grad_tokens.reshape(tokens.shape),
        gain_a.reshape(8),
        sum_qkv,
        gain_qk.reshape(1),
        sum_out,
        gain_f.reshape(8),
        sum_gate_up,
        sum_down,
    )


def solution(mesh):
    placed = (
        P(None, "rows", "ctx", None),
        P(None, "rows", "ctx", None),
        P(None, "rows", None),
        P(None, "rows", "ctx"),
        P(),
        P(),
        P(),
        P(),
        P(),
        P(),
        P(),
    )
    return jax.shard_map(
        local,
        mesh=mesh,
        in_specs=placed,
        out_specs=(
            P(None, "rows", "ctx", None),
            P(None, "rows", "ctx", None),
            P(("rows", "ctx")),
            P(("rows", "ctx"), None),
            P(("rows", "ctx")),
            P(("rows", "ctx"), None),
            P(("rows", "ctx")),
            P(("rows", "ctx"), None),
            P(("rows", "ctx"), None),
        ),
        check_vma=False,
    )
```

profile of v0, /device:TPU:1, one launch (start us, length us, event | category | flops | bytes accessed | tf_op | source)
XLA Modules:
  0.0 144.2 jit_solution(2106233118248201013)
XLA Ops:
  0.6 139.5 %transformer_block.1 = (bf16[256,1024]{1,0:T(8,128)(2,1)}, f32[256,1024]{1,0:T(8,128)}, f32[8,9216]{1,0:T(8,128)}, f32[36,1024]{1,0:T(8,128)}, f32[8,2048]{1,0:T...) custom-call(s32[2,1,5]{2,1,0:T(1,128)} %bounds_ref.1, ...), custom_call_target="tpu_custom_call" | custom-call | tf_op jit(solution)/shard_map/transformer_block/pallas_call | solution.py:1141
  140.2 3.9 %results.1 = (bf16[256,1024]{1,0:T(8,128)(2,1)}, f32[256,1024]{1,0:T(8,128)}, f32[8,9216]{1,0:T(8,128)}, f32[36,1024]{1,0:T(8,128)}, f32[8,2048]{1,0:T(8,128)}, ...) custom-call(bf16[256,1024]{1,0:T(8,128)(2,1)} %get-tuple-element.25.refs_0_, ...), custom_call_target="tpu_custom_call" | custom-call | tf_op jit(solution)/shard_map/results/pallas_call | solution.py:1265
where the time goes:
time: 145 us; the launch traced here: 144 us
  Pallas kernels  143 us (99%)
    pallas_call x1, Pallas kernels, block(): pl.pallas_call(block_kernel, out_shape=(jax.ShapeDtypeStruct((256, 1024),...  140 us
    pallas_call x1, Pallas kernels, finish(): pl.pallas_call(finish_kernel, out_shape=(*same, jax.ShapeDtypeStruct((1,...  3.86 us

commit v1 on v0

--- a/solution.py
+++ b/solution.py
@@ -61,6 +61,16 @@
         return self.at(z=self.z + 1 - 2 * lax.rem(self.z, 2))
 
 
+    def flipped(self, dims):
+        if len(dims) == 1:
+            return self.neighbour(dims[0])
+        if 0 in dims:
+            return self.at(x_hi=1 - self.x_hi)
+        if 2 in dims:
+            return self.at(y=lax.rem(self.y + 2, 4))
+        return self.at(z=lax.rem(self.z + 2, 4))
+
+
 def gray(v):
     return v ^ (v >> 1)
 
@@ -73,92 +83,123 @@
     return sum(((number >> (5 - dim)) & 1) << (5 - t) for t, dim in enumerate(order))
 
 
-HELD_AT = [64 - (64 >> t) for t in range(7)]
+ONES = (1, 1, 1, 1, 1, 1)
+FLIPS = {1: ((1,),), 2: ((0, 1), (1, 0), (1, 1))}
 
 
 class Scatter:
-    def __init__(self, place, orders, first, held, send_sems, recv_sems):
+    def __init__(self, place, orders, shape, first, held, send_sems, recv_sems):
         self.place = place
         self.orders = orders
         self.first, self.first_cols = first
         self.held, self.held_cols = held
         self.send_sems = send_sems
         self.recv_sems = recv_sems
-
-    def part(self, s, t, which):
-        half = 32 >> t
-        if t == 0:
-            return self.first, which * half, self.first_cols
-        return self.held, HELD_AT[t - 1] + which * half, self.held_cols
-
-    def copy(self, s, t):
-        half = 32 >> t
-        dim = self.orders[s][t]
-        ref, start, cols = self.part(s, t, 1 - self.place.bits[dim])
-        return pltpu.make_async_remote_copy(
-            src_ref=ref.at[s, pl.ds(start, half), :, cols],
-            dst_ref=self.held.at[s, pl.ds(HELD_AT[t], half), :, self.held_cols],
-            send_sem=self.send_sems.at[s, t],
-            recv_sem=self.recv_sems.at[s, t],
-            device_id=self.place.neighbour(dim),
-            device_id_type=MESH,
-        )
-
-    def send(self, s, t):
-        self.copy(s, t).start()
-
-    def take(self, s, t):
-        self.copy(s, t).wait_recv()
-        half = 32 >> t
-        ref, start, cols = self.part(s, t, self.place.bits[self.orders[s][t]])
-        per = min(8, half)
+        self.stages = []
+        at, slots, base = 0, 64, 0
+        for width in shape:
+            size = slots >> width
+            self.stages.append((at, width, size, base))
+            base += size * len(FLIPS[width])
+            at += width
+            slots = size
+
+    def source(self, k):
+        if k == 0:
+            return self.first, 0, self.first_cols
+        return self.held, self.stages[k - 1][3], self.held_cols
+
+    def part(self, s, k, flips):
+        at, width, size, _ = self.stages[k]
+        which = 0
+        for dim, flip in zip(self.orders[s][at : at + width], flips, strict=True):
+            bit = self.place.bits[dim]
+            which = 2 * which + (1 - bit if flip else bit)
+        return which * size
+
+    def copies(self, s, k):
+        at, width, size, base = self.stages[k]
+        ref, start, cols = self.source(k)
+        dims = self.orders[s][at : at + width]
+        return [
+            pltpu.make_async_remote_copy(
+                src_ref=ref.at[s, pl.ds(start + self.part(s, k, flips), size), :, cols],
+                dst_ref=self.held.at[s, pl.ds(base + i * size, size), :, self.held_cols],
+                send_sem=self.send_sems.at[min(k, 1)],
+                recv_sem=self.recv_sems.at[s, k],
+                device_id=self.place.flipped([d for d, f in zip(dims, flips, strict=True) if f]),
+                device_id_type=MESH,
+            )
+            for i, flips in enumerate(FLIPS[width])
+        ]
+
+    def send(self, s, k):
+        for copy in self.copies(s, k):
+            copy.start()
+
+    def arrived(self, s, k):
+        _, width, size, base = self.stages[k]
+        place = self.held.at[s, pl.ds(base, size * len(FLIPS[width])), :, self.held_cols]
+        self.wait(place, 0, self.recv_sems.at[s, k]).wait_recv()
+        ref, start, cols = self.source(k)
+        own = start + self.part(s, k, (0,) * width)
+
+        def total(at):
+            value = ref[s, own + at, :, cols].astype(f32)
+            for i in range(len(FLIPS[width])):
+                value = value + self.held[s, base + i * size + at, :, self.held_cols].astype(f32)
+            return value
+
+        return total, size, base
+
+    def take(self, s, k):
+        total, size, base = self.arrived(s, k)
+        per = min(8, size)
 
         def body(i, carry):
             for j in range(per):
                 at = i * per + j
-                self.held[s, HELD_AT[t] + at, :, self.held_cols] = (
-                    self.held[s, HELD_AT[t] + at, :, self.held_cols].astype(f32)
-                    + ref[s, start + at, :, cols].astype(f32)
-                ).astype(bf16)
+                self.held[s, base + at, :, self.held_cols] = total(at).astype(bf16)
             return carry
 
-        lax.fori_loop(0, half // per, body, 0)
-        self.send(s, t + 1)
+        lax.fori_loop(0, size // per, body, 0)
+        self.send(s, k + 1)
 
     def last(self, s):
-        self.copy(s, 5).wait_recv()
-        ref, start, cols = self.part(s, 5, self.place.bits[self.orders[s][5]])
-        return self.held[s, HELD_AT[5], :, self.held_cols].astype(f32) + ref[
-            s, start, :, cols
-        ].astype(f32)
-
-    def sent(self, steps=range(6)):
-        for s in range(6):
-            for t in steps:
-                self.copy(s, t).wait_send()
-
-
-def greet(devices):
-    barrier = pltpu.get_barrier_semaphore()
-    for device in devices:
-        pl.semaphore_signal(barrier, inc=1, device_id=device, device_id_type=MESH)
-    pl.semaphore_wait(barrier, len(devices))
-
-
-def greet_all(place, devices):
+        return self.arrived(s, len(self.stages) - 1)[0](0)
+
+    def wait(self, ref, part, recv_sem):
+        return push(
+            self.place, ref, ref, self.send_sems.at[part], recv_sem, self.place.partner()
+        )
+
+    def sent(self, part):
+        slots = pl.ds(0, 32) if part == 0 else pl.ds(32, 31)
+        self.wait(
+            self.held.at[:, slots, :, self.held_cols], part, self.recv_sems.at[0, 0]
+        ).wait_send()
+
+
+def greet_signal(place, devices):
     barrier = pltpu.get_barrier_semaphore()
     targets = down_targets(place)
     for device in devices + targets[1:]:
         pl.semaphore_signal(barrier, inc=1, device_id=device, device_id_type=MESH)
-    swapped = place.x_hi != place.core
-    count = len(devices) + 3
-
-    @pl.when(swapped)
+
+    @pl.when(place.x_hi != place.core)
     def _():
         pl.semaphore_signal(barrier, inc=1, device_id=targets[0], device_id_type=MESH)
+
+
+def greet_wait(place, devices):
+    barrier = pltpu.get_barrier_semaphore()
+    count = len(devices) + 3
+
+    @pl.when(place.x_hi != place.core)
+    def _():
         pl.semaphore_wait(barrier, count + 1)
 
-    @pl.when(jnp.logical_not(swapped))
+    @pl.when(place.x_hi == place.core)
     def _():
         pl.semaphore_wait(barrier, count)
 
@@ -190,54 +231,55 @@
 
 FF_HALF = 2304
 DOWN_ORDERS = (
-    (1, 3, 5, 2, 0, 4),
-    (4, 0, 1, 3, 5, 2),
-    (0, 1, 3, 2, 4, 5),
-    (5, 3, 0, 1, 2, 4),
-    (3, 2, 4, 5, 1, 0),
-    (2, 3, 5, 0, 4, 1),
+    (1, 5, 4, 2, 3, 0),
+    (0, 2, 5, 1, 3, 4),
+    (4, 3, 1, 0, 2, 5),
+    (0, 2, 1, 3, 5, 4),
+    (5, 3, 2, 0, 1, 4),
+    (2, 3, 1, 4, 5, 0),
 )
 GATE_ORDERS = (
-    (0, 5, 4, 1, 3, 2),
-    (1, 5, 0, 4, 3, 2),
-    (2, 4, 5, 3, 1, 0),
-    (3, 0, 5, 4, 2, 1),
-    (2, 5, 0, 3, 1, 4),
-    (0, 1, 3, 4, 5, 2),
+    (4, 3, 5, 1, 2, 0),
+    (1, 3, 0, 4, 2, 5),
+    (4, 3, 1, 0, 2, 5),
+    (5, 0, 3, 2, 4, 1),
+    (2, 1, 4, 3, 0, 5),
+    (3, 2, 0, 5, 1, 4),
 )
 UP_ORDERS = (
-    (2, 0, 3, 5, 1, 4),
-    (5, 2, 0, 3, 4, 1),
-    (3, 1, 5, 2, 0, 4),
-    (4, 2, 5, 0, 1, 3),
-    (3, 0, 2, 5, 4, 1),
-    (4, 1, 5, 0, 2, 3),
+    (5, 4, 0, 1, 3, 2),
+    (3, 0, 2, 4, 5, 1),
+    (2, 3, 4, 5, 0, 1),
+    (0, 3, 4, 5, 2, 1),
+    (0, 2, 5, 3, 4, 1),
+    (1, 2, 0, 3, 4, 5),
 )
 QUAD_ORDERS = (
-    (1, 2, 0, 5, 4, 3),
-    (0, 4, 1, 2, 3, 5),
-    (3, 1, 5, 0, 2, 4),
-    (2, 0, 3, 4, 1, 5),
-    (2, 4, 3, 5, 0, 1),
-    (4, 0, 2, 3, 5, 1),
+    (4, 5, 0, 1, 3, 2),
+    (0, 1, 2, 3, 5, 4),
+    (5, 4, 3, 2, 1, 0),
+    (1, 0, 4, 5, 3, 2),
+    (2, 3, 1, 0, 4, 5),
+    (3, 2, 5, 4, 1, 0),
 )
+QUAD_STAGES = (1, 1, 2, 2)
+LINKED = ((0,), (1,), (2,), (3,), (4,), (5,), (0, 1), (2, 3), (4, 5))
 STEPS = (
-    "Bmm0", "Amm0", "Bmm2", "dn", "Amm2", "down", "lo", "Amm1", "B40", "datt",
-    "A10", "A40", "A50", "B50", "B10", "out", "Bmm1", "split", "heads0", "D30",
-    "B00", "nat", "A30", "D40", "D50", "heads1", "A20", "A11", "B51", "A00",
-    "D20", "B20", "D10", "D00", "B11", "B30", "A51", "A41", "free", "Qmm4",
-    "Qmm5", "headb", "B52", "B01", "D31", "lastnorm", "B31", "Qmm0", "D41", "D51",
-    "Qmm2", "Qmm3", "D21", "B41", "Qmm1", "D01", "A21", "A31", "v0", "D11",
-    "Q40", "A01", "A42", "D02", "Q50", "v1", "Q00", "Q20", "Q10", "Q30",
-    "B21", "D52", "Q41", "A12", "D32", "B02", "D22", "A22", "B32", "D12",
-    "A43", "A02", "Q51", "v2", "B12", "A52", "B53", "D42", "Q21", "Q11",
-    "A32", "Q31", "Q01", "B22", "B42", "D03", "Q42", "D13", "B03", "D23",
-    "D43", "D53", "A53", "A13", "D33", "A23", "v3", "Q52", "B13", "Q22",
-    "B33", "A03", "Q12", "A33", "Q32", "Q02", "B54", "B43", "B23", "D54",
-    "Q43", "A44", "A14", "D14", "D34", "B14", "v4", "Q53", "Q23", "Q13",
-    "A04", "D44", "Q33", "Q03", "D24", "D04", "A24", "B44", "A54", "B24",
-    "B34", "A34", "B04", "Q24", "v5", "Q54", "Q14", "Q44", "Q34", "Q04",
-    "Dfin", "Afin", "Qfin", "end",
+    "Amm0", "Bmm0", "Bmm1", "Amm1", "Bmm2", "Amm2", "dn", "A10", "down", "B30",
+    "lo", "A50", "A20", "datt", "A00", "A40", "B40", "D20", "B00", "A30",
+    "out", "B50", "D50", "D00", "D10", "B10", "A21", "B31", "split", "heads",
+    "D21", "B01", "B20", "D51", "A31", "free", "B32", "D30", "nat", "A01",
+    "D40", "A41", "A51", "B51", "A22", "Qmm4", "Qmm5", "B41", "B21", "A11",
+    "D11", "headb", "D01", "B11", "D31", "A42", "B02", "lastnorm", "D52", "A02",
+    "Qmm0", "Qmm2", "Qmm1", "Qmm3", "D32", "D41", "B42", "v0", "D02", "B22",
+    "A52", "Q40", "A12", "D22", "A32", "D12", "B52", "D42", "B12", "Q50",
+    "Q20", "Q00", "Q10", "A43", "Q30", "B23", "D33", "v1", "B03", "A13",
+    "D23", "A03", "D43", "A53", "A23", "A33", "B43", "B33", "D13", "B13",
+    "D53", "Q41", "D03", "Q51", "v2", "B53", "Q21", "Q11", "Q01", "A04",
+    "Q31", "D34", "D24", "A44", "B14", "v3", "A14", "B44", "A34", "D14",
+    "A54", "B34", "B24", "A24", "B04", "D04", "D44", "Q52", "B54", "Q42",
+    "D54", "Q22", "Q02", "Q32", "Q12", "v4", "Afin", "Dfin", "Qfin", "v5",
+    "end",
 )
 
 
@@ -256,11 +298,13 @@
                 place,
                 d_stage.at[lax.rem(place.z + off, 4)],
                 d_in.at[place.z],
-                f_send.at[off],
-                f_recv.at[off],
+                f_send.at[min(off, 1)],
+                f_recv.at[min(off, 1)],
                 targets[off],
             )
         )
+    three = d_in.at[pl.ds(0, 3)]
+    others = push(place, three, three, f_send.at[1], f_recv.at[1], targets[1])
     for off in range(1, 4):
         moves[off].start()
 
@@ -273,12 +317,10 @@
     def _():
         d_in[place.z] = d_stage[place.z]
 
-    for off in range(1, 4):
-        moves[off].wait_recv()
+    others.wait_recv()
     for z in range(4):
         gdn_ref[:, pl.ds(256 * z, 256)] = d_in[z, pl.ds(0, 36), :]
-    for off in range(1, 4):
-        moves[off].wait_send()
+    others.wait_send()
 
     @pl.when(swapped)
     def _():
@@ -316,8 +358,9 @@
 
 
 class Exchange:
-    def __init__(self, place, out_at, into_at, send_sems, recv_sems):
+    def __init__(self, place, out_at, into_at, seven, send_sems, recv_sems):
         self.place = place
+        self.seven = seven
         self.out_at = out_at
         self.into_at = into_at
         self.send_sems = send_sems
@@ -329,24 +372,31 @@
             self.place,
             self.out_at(m, j),
             self.into_at(m, self.place.ctx),
-            self.send_sems.at[m, off - 1],
-            self.recv_sems.at[m, off - 1],
+            self.send_sems.at[m],
+            self.recv_sems.at[m],
             (self.place.rows, j),
         )
 
     def send(self, m):
         for off in range(1, 8):
             self.copy(m, off).start()
+        self.keep(m)
+
+    def keep(self, m):
         self.into_at(m, self.place.ctx)[...] = self.out_at(m, self.place.ctx)[...]
 
+    def all_seven(self, m):
+        ref = self.seven(m)
+        return push(
+            self.place, ref, ref, self.send_sems.at[m], self.recv_sems.at[m], self.place.partner()
+        )
+
     def arrived(self, m):
-        for off in range(1, 8):
-            self.copy(m, off).wait_recv()
+        self.all_seven(m).wait_recv()
 
     def sent(self):
         for m in range(2):
-            for off in range(1, 8):
-                self.copy(m, off).wait_send()
+            self.all_seven(m).wait_send()
 
 
 def ctx_peers(place):
@@ -388,11 +438,11 @@
     w_out_hbm,
     out_hbm,
     gtok_hbm,
-    ggu_ref,
-    gdn_ref,
-    gqkv_ref,
-    gout_ref,
-    vec_out,
+    ggu_hbm,
+    gdn_hbm,
+    gqkv_hbm,
+    gout_hbm,
+    vec_hbm,
     na_hbm,
     na_other_hbm,
     att_hbm,
@@ -429,8 +479,13 @@
     q_in,
     vec,
     vec_in,
+    ggu_ref,
+    gdn_ref,
+    gqkv_ref,
+    gout_ref,
     w_sems,
     l_sems,
+    r_sems,
     x_send,
     x_recv,
     a_send,
@@ -459,11 +514,13 @@
     core = place.core
     partner = place.partner()
     every = slice(None)
-    down = Scatter(place, DOWN_ORDERS, (d_first, every), (d_held, every), d_send, d_recv)
-    gate = Scatter(place, GATE_ORDERS, (a_first, every), (a_held, every), a_send, a_recv)
-    up = Scatter(place, UP_ORDERS, (b_first, every), (b_held, every), b_send, b_recv)
+    down = Scatter(place, DOWN_ORDERS, ONES, (d_first, every), (d_held, every), d_send, d_recv)
+    gate = Scatter(place, GATE_ORDERS, ONES, (a_first, every), (a_held, every), a_send, a_recv)
+    up = Scatter(place, UP_ORDERS, ONES, (b_first, every), (b_held, every), b_send, b_recv)
     narrow = pl.ds(0, 256)
-    quad = Scatter(place, QUAD_ORDERS, (a_first, narrow), (b_first, narrow), q_send, q_recv)
+    quad = Scatter(
+        place, QUAD_ORDERS, QUAD_STAGES, (a_first, narrow), (b_first, narrow), q_send, q_recv
+    )
     sums = {"D": down, "A": gate, "B": up, "Q": quad}
     steps = iter(STEPS)
 
@@ -488,6 +545,7 @@
         place,
         lambda m, j: tiles(a_first, m, j, 256),
         lambda m, j: tiles(b_first, m, j, 256),
+        lambda m: b_first.at[m, pl.ds(0, 56), :, pl.ds(0, 256)],
         k_send,
         k_recv,
     )
@@ -495,11 +553,17 @@
         place,
         lambda m, j: tiles(b_first, 4 + m, j, 128),
         lambda m, j: tiles(b_first, 2 + m, j, 128),
+        lambda m: b_first.at[2 + m, pl.ds(0, 56), :, pl.ds(0, 128)],
         e_send,
         e_recv,
     )
     grads_out = Exchange(
-        place, lambda m, j: do_out.at[m, j], lambda m, j: do_in.at[m, j], do_send, do_recv
+        place,
+        lambda m, j: do_out.at[m, j],
+        lambda m, j: do_in.at[m, j],
+        lambda m: do_in.at[m, pl.ds(0, 7)],
+        do_send,
+        do_recv,
     )
     own_rows = pl.ds(0, 256)
     other_rows = pl.ds(256, 256)
@@ -521,16 +585,19 @@
 
     def attend(w_qkv, x_ref, na, proj_ref, q2, kk, vo):
         x_load = pltpu.make_async_copy(x_hbm, x_ref, l_sems.at[2])
-        w_load = pltpu.make_async_copy(w_qkv_hbm, w_qkv, l_sems.at[3])
+        w_loads = [
+            pltpu.make_async_copy(w_qkv_hbm.at[:, cols], w_qkv.at[:, cols], sem)
+            for cols, sem in (
+                (pl.ds(1024, 1024), l_sems.at[3]),
+                (pl.ds(0, 1024), l_sems.at[6]),
+            )
+        ]
         na_copy = pltpu.make_async_copy(na, na_hbm, l_sems.at[4])
         proj_copy = pltpu.make_async_copy(proj_ref, proj_hbm, l_sems.at[5])
-        for load in (x_load, w_load, cot_load):
+        for load in (x_load, *w_loads, cot_load):
             load.start()
-        greet_all(
-            place,
-            [partner] + [place.neighbour(dim) for dim in range(6)] + ctx_peers(place),
-        )
-        to_dy.start()
+        peers = [partner] + [place.flipped(dims) for dims in LINKED] + ctx_peers(place)
+        greet_signal(place, peers)
         columns = jnp.concatenate(
             [pos_ref[0].astype(f32), pos_ref[1].astype(f32), jnp.zeros((6, 128), f32)], 0
         ).T
@@ -545,7 +612,7 @@
         na[...] = (inputs * scale * gain_ref[...]).astype(bf16)
         to_na = push(place, na, na_other_hbm, x_send.at[4], x_recv.at[4], partner)
         na_copy.start()
-        w_load.wait()
+        w_loads[0].wait()
 
         def turned(tile, gain):
             u = tile * lax.rsqrt(head_mean(tile * tile) + norm_eps) * gain
@@ -556,11 +623,6 @@
                 rows = tile[128 * m : 128 * m + 128].astype(bf16)
                 a_first[m, pl.ds(8 * j, 8), :, pl.ds(at, 128)] = rows.reshape(8, 16, 128)
 
-        for i in range(4):
-            pair = dot(na[...], w_qkv[:, pl.ds(256 * i, 256)])
-            proj_ref[:, pl.ds(256 * i, 256)] = pair
-            for j in range(2):
-                store(0, 2 * i + j, turned(pair[:, 128 * j : 128 * j + 128], gain_q) * 0.125)
         for i in range(2):
             key_pair = dot(na[...], w_qkv[:, pl.ds(1024 + 256 * i, 256)])
             value_pair = dot(na[...], w_qkv[:, pl.ds(1536 + 256 * i, 256)])
@@ -570,8 +632,26 @@
                 value = value_pair[:, 128 * j : 128 * j + 128]
                 store(128, 4 * i + 2 * j, jnp.where(low, key, pltpu.roll(value, 64, 1)))
                 store(128, 4 * i + 2 * j + 1, jnp.where(low, pltpu.roll(key, 64, 1), value))
-        for m in range(2):
-            heads_out.send(m)
+        greet_wait(place, peers)
+        to_dy.start()
+
+        w_loads[1].wait()
+        for i in range(4):
+            p = lax.rem(lax.div(place.ctx, 2) + 1 + i, 4)
+            at = pl.ds(pl.multiple_of(256 * p, 256), 256)
+            pair = dot(na[...], w_qkv[:, at])
+            proj_ref[:, at] = pair
+            for j in range(2):
+                store(0, 2 * p + j, turned(pair[:, 128 * j : 128 * j + 128], gain_q) * 0.125)
+            for j in range(2):
+                off = lax.rem(2 * p + j + 8 - place.ctx, 8)
+
+                @pl.when(off > 0)
+                def _(off=off):
+                    heads_out.copy(0, off).start()
+
+        heads_out.keep(0)
+        heads_out.send(1)
         to_na.start()
         proj_copy.start()
 
@@ -684,29 +764,39 @@
         qkv_copy.wait()
         o_copy.wait()
         cot_load.wait()
-        to_dy.wait_recv()
-        to_nf.wait_recv()
+
+        def token_half(half, carry):
+            rows = pl.ds(pl.multiple_of(256 * half, 256), 256)
+
+            @pl.when(half == 1)
+            def _():
+                to_dy.wait_recv()
+                to_nf.wait_recv()
+
+            def units(i, inner):
+                @pl.when(half == 0)
+                def _():
+                    for copy in unit_loads(i):
+                        copy.wait()
+
+                cols = pl.ds(pl.multiple_of(768 * i, 256), 768)
+                up_cols = pl.ds(pl.multiple_of(FF_HALF + 768 * i, 256), 768)
+                gated = dot(nf[rows, :], wgu[:, cols])
+                upward = dot(nf[rows, :], wgu[:, up_cols])
+                grad_hidden = dot_cols(dyb[rows, :], wd[cols, :])
+                sigma = 1.0 / (1.0 + jnp.exp(-gated))
+                silu = gated * sigma
+                h[rows, cols] = (silu * upward).astype(bf16)
+                dgu[rows, cols] = (grad_hidden * upward * (sigma + silu * (1.0 - sigma))).astype(
+                    bf16
+                )
+                dgu[rows, up_cols] = (grad_hidden * silu).astype(bf16)
+                return inner
+
+            return lax.fori_loop(0, 3, units, carry)
+
+        lax.fori_loop(0, 2, token_half, 0)
         nft[:, other_rows] = nf[other_rows, :].T
-
-        def units(i, carry):
-            @pl.when(lax.rem(i, 3) == 0)
-            def _():
-                for copy in unit_loads(lax.div(i, 3)):
-                    copy.wait()
-
-            cols = pl.ds(pl.multiple_of(256 * i, 256), 256)
-            up_cols = pl.ds(pl.multiple_of(FF_HALF + 256 * i, 256), 256)
-            gated = dot(nf[...], wgu[:, cols])
-            upward = dot(nf[...], wgu[:, up_cols])
-            grad_hidden = dot_cols(dyb[...], wd[cols, :])
-            sigma = 1.0 / (1.0 + jnp.exp(-gated))
-            silu = gated * sigma
-            h[:, cols] = (silu * upward).astype(bf16)
-            dgu[:, cols] = (grad_hidden * upward * (sigma + silu * (1.0 - sigma))).astype(bf16)
-            dgu[:, up_cols] = (grad_hidden * silu).astype(bf16)
-            return carry
-
-        lax.fori_loop(0, 9, units, 0)
 
         def down_grads():
             for block in range(3):
@@ -837,7 +927,7 @@
 
     def vec_move(step):
         device = place.neighbour(step) if step < 6 else partner
-        return push(place, vec.at[step], vec_in.at[step], v_send.at[step], v_recv.at[step], device)
+        return push(place, vec.at[step], vec_in.at[step], v_send, v_recv.at[step], device)
 
     def vec_take(step):
         vec_move(step).wait_recv()
@@ -877,12 +967,16 @@
         ]
         for load in loads:
             load.start()
-        grads_back = Exchange(place, lambda m, j: t_out.at[m, j], t_at, t_send, t_recv)
-
-        def heads_grad(m):
-            if m == 0:
-                for load in loads[:2]:
-                    load.wait()
+        grads_back = Exchange(
+            place,
+            lambda m, j: t_out.at[m, j],
+            t_at,
+            lambda m: t_out.at[m, pl.ds(0, 7)],
+            t_send,
+            t_recv,
+        )
+
+        def heads_grad(m, carry):
             grads_out.arrived(m)
             starts = document_edges(bounds_ref, m)[0]
             for b in range(4):
@@ -938,10 +1032,16 @@
                     rows = slice(128 * half, 128 * half + 128)
                     t_out[m, 2 * qb + half, :, pl.ds(0, 128)] = tile[rows]
             grads_back.send(m)
+            return carry
+
+        def heads_grads():
+            for load in loads[:2]:
+                load.wait()
+            lax.fori_loop(0, 2, heads_grad, 0)
 
         def sums_free():
-            gate.sent([0])
-            up.sent([0])
+            gate.sent(0)
+            up.sent(0)
             for dim in range(6):
                 pl.semaphore_signal(
                     free_sem, inc=1, device_id=place.neighbour(dim), device_id_type=MESH
@@ -1054,8 +1154,7 @@
             vec_move(0).start()
 
         ops = {
-            "heads0": functools.partial(heads_grad, 0),
-            "heads1": functools.partial(heads_grad, 1),
+            "heads": heads_grads,
             "free": sums_free,
             "nat": token_sides,
             "headb": turn_back,
@@ -1106,11 +1205,28 @@
             return gqkv_ref, pl.ds(pl.multiple_of(of * 1024 + 256 * s, 256), 256)
         return gout_ref, pl.ds(pl.multiple_of(of * 512 + 256 * (s - 4), 256), 256)
 
+    results = [
+        pltpu.make_async_copy(source, target, r_sems.at[i])
+        for i, (source, target) in enumerate(
+            (
+                (gdn_ref, gdn_hbm),
+                (ggu_ref, ggu_hbm),
+                (gqkv_ref, gqkv_hbm),
+                (gout_ref, gout_hbm),
+                (vec.at[7], vec_hbm),
+            )
+        )
+    ]
+    results[0].start()
     for s in range(12):
         ggu_ref[:, wide_cols(core, s)] = g_fin[core, s]
     swap.wait_recv()
     for s in range(12):
         ggu_ref[:, wide_cols(1 - core, s)] = g_in[s]
+    results[1].start()
+    vec_move(6).wait_recv()
+    vec[7] = vec[6] + vec_in[6]
+    results[4].start()
     for s in range(6):
         ref, at = quad_cols(core, s)
         ref[:, at] = q_fin[core, s]
@@ -1118,19 +1234,19 @@
     for s in range(6):
         ref, at = quad_cols(1 - core, s)
         ref[:, at] = q_in[s]
-    vec_move(6).wait_recv()
-    vec_out[...] = vec[6] + vec_in[6]
+    results[2].start()
+    results[3].start()
 
     for move in (to_dy, to_dm, swap, swap_q):
         move.wait_send()
     out_copy.wait()
-    for step in range(7):
-        vec_move(step).wait_send()
-    down.sent()
-    gate.sent(range(1, 6))
-    up.sent(range(1, 6))
-    quad.sent()
+    push(place, vec_in, vec_in, v_send, v_recv.at[0], partner).wait_send()
+    for scatter, parts in ((down, (0, 1)), (gate, (1,)), (up, (1,)), (quad, (0, 1))):
+        for part in parts:
+            scatter.sent(part)
     grads_out.sent()
+    for copy in results:
+        copy.wait()
 
 
 def block(bounds, *arrays):
@@ -1157,7 +1273,7 @@
             jax.ShapeDtypeStruct((2, 64, 16, 128), bf16),
         ),
         in_specs=[smem] + [vmem] * 5 + [hbm] * 6,
-        out_specs=(hbm, hbm) + (vmem,) * 5 + (hbm,) * 7,
+        out_specs=(hbm,) * 14,
         scratch_shapes=[
             pltpu.VMEM((6, 64, 16, 384), bf16),
             pltpu.VMEM((6, 63, 16, 384), bf16),
@@ -1186,31 +1302,36 @@
             pltpu.VMEM((4, 40, 256), f32),
             pltpu.VMEM((2, 6, 8, 256), f32),
             pltpu.VMEM((6, 8, 256), f32),
+            pltpu.VMEM((8, 24, 128), f32),
             pltpu.VMEM((7, 24, 128), f32),
-            pltpu.VMEM((7, 24, 128), f32),
+            pltpu.VMEM((8, 9216), f32),
+            pltpu.VMEM((36, 1024), f32),
+            pltpu.VMEM((8, 2048), f32),
+            pltpu.VMEM((8, 1024), f32),
             dma((9,)),
             dma((10,)),
+            dma((5,)),
             dma((10,)),
             dma((10,)),
+            dma((2,)),
             dma((6, 6)),
+            dma((2,)),
             dma((6, 6)),
+            dma((2,)),
             dma((6, 6)),
-            dma((6, 6)),
-            dma((6, 6)),
-            dma((6, 6)),
-            dma((6, 6)),
-            dma((6, 6)),
-            dma((4,)),
-            dma((4,)),
-            dma((2, 7)),
-            dma((2, 7)),
-            dma((2, 7)),
-            dma((2, 7)),
-            dma((2, 7)),
-            dma((2, 7)),
-            dma((2, 7)),
-            dma((2, 7)),
-            dma((7,)),
+            dma((2,)),
+            dma((6, 4)),
+            dma((2,)),
+            dma((2,)),
+            dma((2,)),
+            dma((2,)),
+            dma((2,)),
+            dma((2,)),
+            dma((2,)),
+            dma((2,)),
+            dma((2,)),
+            dma((2,)),
+            dma,
             dma((7,)),
             pltpu.SemaphoreType.REGULAR,
         ],

time: 145 us -> 138 us (0.952)
  Pallas kernels: 143 us -> 137 us
    pallas_call x1, Pallas kernels: 140 us -> 133 us  [block(): pl.pallas_call(block_kernel, out_shape=(jax.ShapeDtypeStruct((256, 1024),...]
where the time goes in v1:
time: 138 us
  Pallas kernels  137 us (99%)
    pallas_call x1, Pallas kernels, block(): pl.pallas_call(block_kernel, out_shape=(jax.ShapeDtypeStruct((256, 1024),...  133 us
    pallas_call x1, Pallas kernels, finish(): pl.pallas_call(finish_kernel, out_shape=(*same, jax.ShapeDtypeStruct((1,...  3.86 us

profile of v1, /device:TPU:1, one launch (start us, length us, event | category | flops | bytes accessed | tf_op | source)
XLA Modules:
  0.0 137.9 jit_solution(10575914977517900432)
XLA Ops:
  0.6 133.2 %transformer_block.1 = (bf16[256,1024]{1,0:T(8,128)(2,1)}, f32[256,1024]{1,0:T(8,128)}, f32[8,9216]{1,0:T(8,128)}, f32[36,1024]{1,0:T(8,128)}, f32[8,2048]{1,0:T...) custom-call(s32[2,1,5]{2,1,0:T(1,128)} %bounds_ref.1, ...), custom_call_target="tpu_custom_call" | custom-call | tf_op jit(solution)/shard_map/transformer_block/pallas_call | solution.py:1257
  133.9 3.9 %results.1 = (bf16[256,1024]{1,0:T(8,128)(2,1)}, f32[256,1024]{1,0:T(8,128)}, f32[8,9216]{1,0:T(8,128)}, f32[36,1024]{1,0:T(8,128)}, f32[8,2048]{1,0:T(8,128)}, ...) custom-call(bf16[256,1024]{1,0:T(8,128)(2,1)} %get-tuple-element.25.refs_0_, ...), custom_call_target="tpu_custom_call" | custom-call | tf_op jit(solution)/shard_map/results/pallas_call | solution.py:1386

commit v2 on v1

--- a/solution.py
+++ b/solution.py
@@ -231,100 +231,111 @@
 
 FF_HALF = 2304
 DOWN_ORDERS = (
-    (1, 5, 4, 2, 3, 0),
-    (0, 2, 5, 1, 3, 4),
-    (4, 3, 1, 0, 2, 5),
-    (0, 2, 1, 3, 5, 4),
-    (5, 3, 2, 0, 1, 4),
-    (2, 3, 1, 4, 5, 0),
+    (0, 3, 5, 2, 1, 4),
+    (3, 5, 4, 2, 0, 1),
+    (2, 3, 0, 4, 1, 5),
+    (4, 2, 0, 1, 3, 5),
+    (5, 2, 3, 4, 0, 1),
+    (0, 3, 4, 1, 5, 2),
 )
 GATE_ORDERS = (
-    (4, 3, 5, 1, 2, 0),
-    (1, 3, 0, 4, 2, 5),
-    (4, 3, 1, 0, 2, 5),
-    (5, 0, 3, 2, 4, 1),
+    (5, 2, 1, 3, 4, 0),
+    (4, 0, 3, 5, 1, 2),
     (2, 1, 4, 3, 0, 5),
-    (3, 2, 0, 5, 1, 4),
+    (0, 3, 2, 5, 4, 1),
+    (4, 0, 2, 3, 5, 1),
+    (5, 3, 0, 2, 1, 4),
 )
 UP_ORDERS = (
-    (5, 4, 0, 1, 3, 2),
-    (3, 0, 2, 4, 5, 1),
-    (2, 3, 4, 5, 0, 1),
-    (0, 3, 4, 5, 2, 1),
-    (0, 2, 5, 3, 4, 1),
-    (1, 2, 0, 3, 4, 5),
+    (2, 3, 1, 4, 0, 5),
+    (3, 4, 5, 0, 2, 1),
+    (0, 2, 5, 4, 3, 1),
+    (1, 0, 2, 3, 5, 4),
+    (1, 2, 5, 0, 4, 3),
+    (3, 1, 2, 0, 4, 5),
 )
 QUAD_ORDERS = (
-    (4, 5, 0, 1, 3, 2),
-    (0, 1, 2, 3, 5, 4),
+    (2, 3, 1, 0, 4, 5),
+    (1, 0, 5, 4, 2, 3),
+    (3, 2, 1, 0, 5, 4),
     (5, 4, 3, 2, 1, 0),
-    (1, 0, 4, 5, 3, 2),
-    (2, 3, 1, 0, 4, 5),
-    (3, 2, 5, 4, 1, 0),
+    (4, 5, 2, 3, 0, 1),
+    (1, 0, 5, 4, 2, 3),
 )
 QUAD_STAGES = (1, 1, 2, 2)
 LINKED = ((0,), (1,), (2,), (3,), (4,), (5,), (0, 1), (2, 3), (4, 5))
 STEPS = (
-    "Amm0", "Bmm0", "Bmm1", "Amm1", "Bmm2", "Amm2", "dn", "A10", "down", "B30",
-    "lo", "A50", "A20", "datt", "A00", "A40", "B40", "D20", "B00", "A30",
-    "out", "B50", "D50", "D00", "D10", "B10", "A21", "B31", "split", "heads",
-    "D21", "B01", "B20", "D51", "A31", "free", "B32", "D30", "nat", "A01",
-    "D40", "A41", "A51", "B51", "A22", "Qmm4", "Qmm5", "B41", "B21", "A11",
-    "D11", "headb", "D01", "B11", "D31", "A42", "B02", "lastnorm", "D52", "A02",
-    "Qmm0", "Qmm2", "Qmm1", "Qmm3", "D32", "D41", "B42", "v0", "D02", "B22",
-    "A52", "Q40", "A12", "D22", "A32", "D12", "B52", "D42", "B12", "Q50",
-    "Q20", "Q00", "Q10", "A43", "Q30", "B23", "D33", "v1", "B03", "A13",
-    "D23", "A03", "D43", "A53", "A23", "A33", "B43", "B33", "D13", "B13",
-    "D53", "Q41", "D03", "Q51", "v2", "B53", "Q21", "Q11", "Q01", "A04",
-    "Q31", "D34", "D24", "A44", "B14", "v3", "A14", "B44", "A34", "D14",
-    "A54", "B34", "B24", "A24", "B04", "D04", "D44", "Q52", "B54", "Q42",
-    "D54", "Q22", "Q02", "Q32", "Q12", "v4", "Afin", "Dfin", "Qfin", "v5",
+    "Bmm0", "Amm0", "Bmm1", "Bmm2", "Amm2", "Amm1", "dn", "B00", "down", "lo",
+    "B20", "A20", "A00", "A10", "B30", "datt", "B50", "A40", "B10", "B40",
+    "A30", "D40", "D10", "out", "A21", "B01", "A50", "split", "D20", "B21",
+    "heads", "A31", "nat", "D00", "B51", "B11", "free", "D11", "A11", "D21",
+    "D30", "A01", "A22", "D50", "B41", "D41", "B02", "B22", "A51", "B31",
+    "Qmm4", "B52", "Qmm5", "A12", "D01", "A32", "headb", "A41", "lastnorm", "A02",
+    "D12", "B03", "B12", "D31", "D51", "B23", "B32", "Qmm0", "Qmm1", "Qmm3",
+    "Qmm2", "D42", "B53", "A13", "v0", "D13", "B24", "A42", "A23", "A52",
+    "B42", "Q50", "A33", "B13", "A03", "D02", "B04", "D22", "D32", "D14",
+    "Q40", "A24", "D52", "B33", "B43", "D43", "Q00", "B54", "Q10", "Q30",
+    "v1", "Q20", "A53", "A34", "Q51", "B14", "A04", "D23", "D33", "D03",
+    "A43", "D53", "v2", "Q41", "B44", "A54", "Q01", "B34", "Q11", "A14",
+    "Q31", "Q21", "D04", "D34", "v3", "Q52", "D54", "D24", "A44", "D44",
+    "Q42", "Q02", "Q12", "Q32", "Q22", "v4", "Afin", "Dfin", "Qfin", "v5",
     "end",
 )
 
 
-def finish_down(place, down, d_acc, d_stage, d_in, f_send, f_recv, gdn_ref):
-    for s in range(6):
-        d_acc[pl.ds(48 * (s // 2), 48), pl.ds(128 * (s % 2), 128)] = down.last(s)
-    for z in range(4):
-        d_stage[z, pl.ds(0, 36), :] = d_acc[pl.ds(36 * z, 36), :]
-        d_stage[z, pl.ds(36, 4), :] = jnp.zeros((4, 256), f32)
-    targets = down_targets(place)
-    swapped = place.x_hi != place.core
-    moves = []
-    for off in range(4):
-        moves.append(
+class DownOwners:
+    def __init__(self, place, stage, into, send_sems, recv_sems):
+        self.swapped = place.x_hi != place.core
+        self.place = place
+        self.stage = stage
+        self.into = into
+        targets = down_targets(place)
+        self.moves = [
             push(
                 place,
-                d_stage.at[lax.rem(place.z + off, 4)],
-                d_in.at[place.z],
-                f_send.at[min(off, 1)],
-                f_recv.at[min(off, 1)],
+                stage.at[lax.rem(place.z + off, 4)],
+                into.at[place.z],
+                send_sems.at[min(off, 1)],
+                recv_sems.at[min(off, 1)],
                 targets[off],
             )
-        )
-    three = d_in.at[pl.ds(0, 3)]
-    others = push(place, three, three, f_send.at[1], f_recv.at[1], targets[1])
-    for off in range(1, 4):
-        moves[off].start()
-
-    @pl.when(swapped)
-    def _():
-        moves[0].start()
-        moves[0].wait_recv()
-
-    @pl.when(jnp.logical_not(swapped))
-    def _():
-        d_in[place.z] = d_stage[place.z]
-
-    others.wait_recv()
-    for z in range(4):
-        gdn_ref[:, pl.ds(256 * z, 256)] = d_in[z, pl.ds(0, 36), :]
-    others.wait_send()
-
-    @pl.when(swapped)
-    def _():
-        moves[0].wait_send()
+            for off in range(4)
+        ]
+        three = into.at[pl.ds(0, 3)]
+        self.others = push(place, three, three, send_sems.at[1], recv_sems.at[1], targets[1])
+
+    def send(self, down, acc):
+        for s in range(6):
+            acc[pl.ds(48 * (s // 2), 48), pl.ds(128 * (s % 2), 128)] = down.last(s)
+        for z in range(4):
+            self.stage[z, pl.ds(0, 36), :] = acc[pl.ds(36 * z, 36), :]
+            self.stage[z, pl.ds(36, 4), :] = jnp.zeros((4, 256), f32)
+        for move in self.moves[1:]:
+            move.start()
+
+        @pl.when(self.swapped)
+        def _():
+            self.moves[0].start()
+
+        @pl.when(jnp.logical_not(self.swapped))
+        def _():
+            self.into[self.place.z] = self.stage[self.place.z]
+
+    def arrived(self, out):
+        @pl.when(self.swapped)
+        def _():
+            self.moves[0].wait_recv()
+
+        self.others.wait_recv()
+        for z in range(4):
+            out[:, pl.ds(256 * z, 256)] = self.into[z, pl.ds(0, 36), :]
+
+    def sent(self):
+        self.others.wait_send()
+
+        @pl.when(self.swapped)
+        def _():
+            self.moves[0].wait_send()
 
 
 def lanes(rows):
@@ -816,15 +827,11 @@
                 down.send(s, 0)
 
         def back_to_norm():
-            def pair(i, carry):
-                for j in range(2):
-                    at = pl.ds(pl.multiple_of(512 * i + 256 * j, 256), 256)
-                    part = dot_cols(dgu[...], wgu[at, :])
-                    dmid[:, at] = part[:256]
-                    sum_send[:, at] = part[256:].astype(bf16)
-                return carry
-
-            lax.fori_loop(0, 2, pair, 0)
+            for j in range(4):
+                at = pl.ds(256 * j, 256)
+                part = dot_cols(dgu[...], wgu[at, :])
+                dmid[:, at] = part[:256]
+                sum_send[:, at] = part[256:].astype(bf16)
             to_back.start()
 
         def wide_grads(scatter, first, base, orders, p):
@@ -934,8 +941,10 @@
         vec[step + 1] = vec[step] + vec_in[step]
         vec_move(step + 1).start()
 
+    down_out = DownOwners(place, d_stage, d_in, f_send, f_recv)
+
     def down_end():
-        finish_down(place, down, d_acc, d_stage, d_in, f_send, f_recv, gdn_ref)
+        down_out.send(down, d_acc)
 
     swap = push(place, g_fin.at[1 - core], g_in, x_send.at[8], x_recv.at[8], partner)
     swap_q = push(place, q_fin.at[1 - core], q_in, x_send.at[9], x_recv.at[9], partner)
@@ -1217,9 +1226,10 @@
             )
         )
     ]
-    results[0].start()
     for s in range(12):
         ggu_ref[:, wide_cols(core, s)] = g_fin[core, s]
+    down_out.arrived(gdn_ref)
+    results[0].start()
     swap.wait_recv()
     for s in range(12):
         ggu_ref[:, wide_cols(1 - core, s)] = g_in[s]
@@ -1245,6 +1255,7 @@
         for part in parts:
             scatter.sent(part)
     grads_out.sent()
+    down_out.sent()
     for copy in results:
         copy.wait()
 
@@ -1346,13 +1357,18 @@
     arrays, vec = refs[:6], refs[6]
     targets, (gain_a, gain_f, gain_qk) = refs[7:13], refs[13:16]
     passing, (in_sems, out_sems) = refs[16:22], refs[22:]
+    pieces = [
+        (source, held, target, pl.ds(first, min(64, source.shape[0])))
+        for source, held, target in zip(arrays, passing, targets, strict=True)
+        for first in range(0, source.shape[0], 64)
+    ]
     reads = [
-        pltpu.make_async_copy(array, held, in_sems.at[i])
-        for i, (array, held) in enumerate(zip(arrays, passing, strict=True))
+        pltpu.make_async_copy(source.at[rows], held.at[rows], in_sems.at[i])
+        for i, (source, held, _, rows) in enumerate(pieces)
     ]
     writes = [
-        pltpu.make_async_copy(held, target, out_sems.at[i])
-        for i, (held, target) in enumerate(zip(passing, targets, strict=True))
+        pltpu.make_async_copy(held.at[rows], target.at[rows], out_sems.at[i])
+        for i, (_, held, target, rows) in enumerate(pieces)
     ]
     for read in reads:
         read.start()
@@ -1394,7 +1410,7 @@
         in_specs=[hbm] * 6 + [vmem],
         out_specs=(hbm,) * 6 + (vmem,) * 3,
         scratch_shapes=[pltpu.VMEM(a.shape, a.dtype) for a in same]
-        + [pltpu.SemaphoreType.DMA((6,)), pltpu.SemaphoreType.DMA((6,))],
+        + [pltpu.SemaphoreType.DMA((12,)), pltpu.SemaphoreType.DMA((12,))],
         name="results",
     )(out, gtok, ggu, gdn, gqkv, gout, vec)
 

time: 138 us -> 138 us (level)
  no operation moved by 1% of the time
where the time goes in v2:
time: 138 us
  Pallas kernels  137 us (99%)
    pallas_call x1, Pallas kernels, block(): pl.pallas_call(block_kernel, out_shape=(jax.ShapeDtypeStruct((256, 1024),...  133 us
    pallas_call x1, Pallas kernels, finish(): pl.pallas_call(finish_kernel, out_shape=(*same, jax.ShapeDtypeStruct((1,...  3.79 us

profile of v2, /device:TPU:1, one launch (start us, length us, event | category | flops | bytes accessed | tf_op | source)
XLA Modules:
  0.0 137.6 jit_solution(6909410083129762185)
XLA Ops:
  0.6 132.9 %transformer_block.1 = (bf16[256,1024]{1,0:T(8,128)(2,1)}, f32[256,1024]{1,0:T(8,128)}, f32[8,9216]{1,0:T(8,128)}, f32[36,1024]{1,0:T(8,128)}, f32[8,2048]{1,0:T...) custom-call(s32[2,1,5]{2,1,0:T(1,128)} %bounds_ref.1, ...), custom_call_target="tpu_custom_call" | custom-call | tf_op jit(solution)/shard_map/transformer_block/pallas_call | solution.py:1268
  133.6 3.8 %results.1 = (bf16[256,1024]{1,0:T(8,128)(2,1)}, f32[256,1024]{1,0:T(8,128)}, f32[8,9216]{1,0:T(8,128)}, f32[36,1024]{1,0:T(8,128)}, f32[8,2048]{1,0:T(8,128)}, ...) custom-call(bf16[256,1024]{1,0:T(8,128)(2,1)} %get-tuple-element.25.refs_0_, ...), custom_call_target="tpu_custom_call" | custom-call | tf_op jit(solution)/shard_map/results/pallas_call | solution.py:1402

commit v3 on v2

--- a/solution.py
+++ b/solution.py
@@ -154,12 +154,18 @@
 
     def take(self, s, k):
         total, size, base = self.arrived(s, k)
-        per = min(8, size)
+        ref, start, cols = self.source(k)
+        own = start + self.part(s, k, (0,) * self.stages[k][1])
+        per = min(16, size)
 
         def body(i, carry):
             for j in range(per):
                 at = i * per + j
-                self.held[s, base + at, :, self.held_cols] = total(at).astype(bf16)
+                if self.stages[k][1] == 1:
+                    value = ref[s, own + at, :, cols] + self.held[s, base + at, :, self.held_cols]
+                else:
+                    value = total(at).astype(bf16)
+                self.held[s, base + at, :, self.held_cols] = value
             return carry
 
         lax.fori_loop(0, size // per, body, 0)

time: 138 us -> 137 us (level)
  no operation moved by 1% of the time
where the time goes in v3:
time: 137 us; the launch traced here: 136 us
  Pallas kernels  136 us (99%)
    pallas_call x1, Pallas kernels, block(): pl.pallas_call(block_kernel, out_shape=(jax.ShapeDtypeStruct((256, 1024),...  132 us
    pallas_call x1, Pallas kernels, finish(): pl.pallas_call(finish_kernel, out_shape=(*same, jax.ShapeDtypeStruct((1,...  3.79 us

profile of v3, /device:TPU:1, one launch (start us, length us, event | category | flops | bytes accessed | tf_op | source)
XLA Modules:
  0.0 136.5 jit_solution(17383724261970120765)
XLA Ops:
  0.6 131.8 %transformer_block.1 = (bf16[256,1024]{1,0:T(8,128)(2,1)}, f32[256,1024]{1,0:T(8,128)}, f32[8,9216]{1,0:T(8,128)}, f32[36,1024]{1,0:T(8,128)}, f32[8,2048]{1,0:T...) custom-call(s32[2,1,5]{2,1,0:T(1,128)} %bounds_ref.1, ...), custom_call_target="tpu_custom_call" | custom-call | tf_op jit(solution)/shard_map/transformer_block/pallas_call | solution.py:1274
  132.5 3.8 %results.1 = (bf16[256,1024]{1,0:T(8,128)(2,1)}, f32[256,1024]{1,0:T(8,128)}, f32[8,9216]{1,0:T(8,128)}, f32[36,1024]{1,0:T(8,128)}, f32[8,2048]{1,0:T(8,128)}, ...) custom-call(bf16[256,1024]{1,0:T(8,128)(2,1)} %get-tuple-element.25.refs_0_, ...), custom_call_target="tpu_custom_call" | custom-call | tf_op jit(solution)/shard_map/results/pallas_call | solution.py:1408

commit v4 on v3

--- a/solution.py
+++ b/solution.py
@@ -864,16 +864,11 @@
 
         def output():
             to_back.wait_send()
-
-            def pair(i, carry):
-                for j in range(2):
-                    at = pl.ds(pl.multiple_of(512 * i + 256 * j, 256), 256)
-                    part = dot(h[...], wd[:, at])
-                    sum_own[:, at] = part[:256]
-                    sum_send[:, at] = part[256:].astype(bf16)
-                return carry
-
-            lax.fori_loop(0, 2, pair, 0)
+            for j in range(4):
+                at = pl.ds(256 * j, 256)
+                part = dot(h[...], wd[:, at])
+                sum_own[:, at] = part[:256]
+                sum_send[:, at] = part[256:].astype(bf16)
             to_out.start()
             w_out_load.start()
 
@@ -1121,16 +1116,12 @@
             for m in range(2):
                 grads_back.arrived(m)
             sum_k = jnp.zeros((1, 128), f32)
-
-            def query_pair(i, total):
-                for j in range(2):
-                    at = pl.ds(pl.multiple_of(256 * i + 128 * j, 128), 128)
-                    back, part = head_back(both_rows(2 * i + j, 0), proj_ref[:, at], gain_q)
-                    dp[0, :, at] = back.astype(bf16)
-                    total = total + part
-                return total
-
-            sum_q = lax.fori_loop(0, 4, query_pair, jnp.zeros((1, 128), f32))
+            sum_q = jnp.zeros((1, 128), f32)
+            for j in range(8):
+                at = pl.ds(128 * j, 128)
+                back, part = head_back(both_rows(j, 0), proj_ref[:, at], gain_q)
+                dp[0, :, at] = back.astype(bf16)
+                sum_q = sum_q + part
             for i in range(4):
                 first = both_rows(2 * i, 128)
                 second = both_rows(2 * i + 1, 128)

time: 137 us -> 136 us (level)
  no operation moved by 1% of the time
where the time goes in v4:
time: 136 us
  Pallas kernels  135 us (99%)
    pallas_call x1, Pallas kernels, block(): pl.pallas_call(block_kernel, out_shape=(jax.ShapeDtypeStruct((256, 1024),...  131 us
    pallas_call x1, Pallas kernels, finish(): pl.pallas_call(finish_kernel, out_shape=(*same, jax.ShapeDtypeStruct((1,...  3.79 us

profile of v4, /device:TPU:1, one launch (start us, length us, event | category | flops | bytes accessed | tf_op | source)
XLA Modules:
  0.0 135.9 jit_solution(4597684939741184455)
XLA Ops:
  0.6 131.2 %transformer_block.1 = (bf16[256,1024]{1,0:T(8,128)(2,1)}, f32[256,1024]{1,0:T(8,128)}, f32[8,9216]{1,0:T(8,128)}, f32[36,1024]{1,0:T(8,128)}, f32[8,2048]{1,0:T...) custom-call(s32[2,1,5]{2,1,0:T(1,128)} %bounds_ref.1, ...), custom_call_target="tpu_custom_call" | custom-call | tf_op jit(solution)/shard_map/transformer_block/pallas_call | solution.py:1265
  131.9 3.8 %results.1 = (bf16[256,1024]{1,0:T(8,128)(2,1)}, f32[256,1024]{1,0:T(8,128)}, f32[8,9216]{1,0:T(8,128)}, f32[36,1024]{1,0:T(8,128)}, f32[8,2048]{1,0:T(8,128)}, ...) custom-call(bf16[256,1024]{1,0:T(8,128)(2,1)} %get-tuple-element.25.refs_0_, ...), custom_call_target="tpu_custom_call" | custom-call | tf_op jit(solution)/shard_map/results/pallas_call | solution.py:1399
